TPU v7x, 128 devices: a whole 4x4x4 slice. The times are simulated.
128 devices in a mesh: phase: 2 (over core), dp: 32 (over z, y, x_lo), mp: 2 (over x_hi).
Axes of the slice: x: 4 (x_hi: 2, x_lo: 2; x = x_hi * 2 + x_lo), y: 4, z: 4, core: 2. Of those that a mesh axis runs over, the one named last changes fastest.
Arguments:
- segments: bfloat16 [2, 64, 64, 4096], P(None, 'dp', 'mp'), may hold values from -6 to 6
- memory_in: bfloat16 [64, 64, 4096], P('dp', 'mp'), may hold values from -6 to 6
- seg_lengths: int32 [2, 64], P(None, 'dp'), may hold values from 1 to 64, as said below
- routes: int32 [2, 32], replicated, may hold values from 0 to 31, each once within a row
- w_query: bfloat16 [2, 4096, 4096], P('phase', None, 'mp'), may hold values from -12 to 12
- w_key: bfloat16 [2, 4096, 1024], P('phase', None, 'mp'), may hold values from -1 to 1
- value_weight: bfloat16 [2, 4096, 1024], P('phase', None, 'mp'), may hold values from -0.09375 to 0.09375
- w_out: bfloat16 [2, 4096, 4096], P('phase', 'mp'), may hold values from -0.09375 to 0.09375
- norm_gain: bfloat16 [2, 4096], P('phase'), may hold values from 0.099609375 to 1.8984375
Outputs:
- mem_states: bfloat16 [2, 2, 64, 64, 4096], P('phase', None, 'dp', 'mp')
- seg_states: bfloat16 [2, 2, 64, 64, 4096], P('phase', None, 'dp', 'mp')
Inputs may be any that keep to these rules, and one draw needn't show every extreme that they name: Each row m is a permutation of the data groups: slot m of group g hands its memory to slot m of group routes[m, g]. `seg_lengths`: some entry equals 64.
All inputs are finite; a program needn't handle non-finite values.
Results may differ from a plain program's by a relative error of at most 0.025.
Values may be sent and summed in bfloat16 or wider, within the bound.
A program may use at most 192 MiB of HBM per device.

v0:
```python
import jax
import jax.numpy as jnp
from jax import lax
from jax.sharding import PartitionSpec as P

HEAD_SIZE = 128


EPSILON = 1e-05


def shifted(value, axis, steps):
    count = lax.axis_size(axis)
    pairs = [(source, (source + steps) % count) for source in range(count)]
    return lax.ppermute(value, axis, pairs)


def norm_rows(rows, gain):
    values = rows.astype(jnp.float32)
    scaled = values * lax.rsqrt(jnp.mean(values * values, axis=-1, keepdims=True) + EPSILON)
    return (scaled * gain.astype(jnp.float32)).astype(jnp.bfloat16)


def section_layer(mem_x, seg_x, length, w_query, w_key, value_weight, w_out, gain):
    mem_dev = mem_x.shape[0]
    seg_dev = seg_x.shape[0]
    all_mem, all_seg = (
        lax.all_gather(norm_rows(mem_x, gain), "mp", axis=0, tiled=True),
        lax.all_gather(norm_rows(seg_x, gain), "mp", axis=0, tiled=True),
    )
    mem_rows = all_mem.shape[0]
    normed = jnp.concatenate([all_mem, all_seg], axis=0)
    rows_total = normed.shape[0]
    kv_dev = w_key.shape[1] // HEAD_SIZE
    query_dev = w_query.shape[1] // HEAD_SIZE
    per_group = query_dev // kv_dev
    heads_of_query = jnp.dot(normed, w_query, preferred_element_type=jnp.float32).astype(
        jnp.bfloat16
    )
    heads_of_query = heads_of_query.reshape(rows_total, kv_dev, per_group, HEAD_SIZE)
    heads_of_key = jnp.dot(normed, w_key, preferred_element_type=jnp.float32).astype(jnp.bfloat16)
    heads_of_key = heads_of_key.reshape(rows_total, kv_dev, HEAD_SIZE)
    heads_of_value = jnp.dot(normed, value_weight, preferred_element_type=jnp.float32).astype(
        jnp.bfloat16
    )
    heads_of_value = heads_of_value.reshape(rows_total, kv_dev, HEAD_SIZE)
    scores = jnp.einsum(
        "qcgd,kcd->cgqk", heads_of_query, heads_of_key, preferred_element_type=jnp.float32
    ) * HEAD_SIZE ** (-0.5)
    query_pos = lax.broadcasted_iota(jnp.int32, (rows_total, rows_total), 0)
    key_pos = lax.broadcasted_iota(jnp.int32, (rows_total, rows_total), 1)
    visible = (key_pos < mem_rows) | (key_pos - mem_rows < length) & (
        (query_pos < mem_rows) | (key_pos <= query_pos)
    )
    scores = jnp.where(visible, scores, -1e30)
    row_max = jnp.max(scores, axis=-1, keepdims=True)
    exponent = jnp.exp(scores - row_max)
    attn = (exponent / jnp.sum(exponent, axis=-1, keepdims=True)).astype(jnp.bfloat16)
    attended = jnp.einsum(
        "cgqk,kcd->qcgd", attn, heads_of_value, preferred_element_type=jnp.float32
    )
    attended = attended.astype(jnp.bfloat16).reshape(rows_total, query_dev * HEAD_SIZE)
    attended_mem = attended[:mem_rows]
    attended_seg = attended[mem_rows:]
    block_rows = mem_dev + seg_dev
    blocks = block_rows * lax.axis_size("mp") // block_rows
    term_mem = jnp.dot(attended_mem, w_out, preferred_element_type=jnp.float32).reshape(
        blocks, mem_dev, -1
    )
    term_seg = jnp.dot(attended_seg, w_out, preferred_element_type=jnp.float32).reshape(
        blocks, seg_dev, -1
    )
    summed = lax.psum_scatter(
        jnp.concatenate([term_mem, term_seg], axis=1)
        .reshape(block_rows * lax.axis_size("mp"), -1)
        .astype(jnp.bfloat16),
        "mp",
        scatter_dimension=0,
        tiled=True,
    ).astype(jnp.float32)
    new_mem = (mem_x.astype(jnp.float32) + summed[:mem_dev]).astype(jnp.bfloat16)
    new_seg = (seg_x.astype(jnp.float32) + summed[mem_dev:]).astype(jnp.bfloat16)
    return (new_mem, new_seg)


def route_memory(arrived, perm_row, group_index):
    group_count = perm_row.shape[0]
    group_ids = jnp.arange(group_count, dtype=jnp.int32)
    target = jnp.sum(jnp.where(group_ids == group_index, perm_row, 0))
    outgoing = jnp.where(
        (group_ids == target)[:, None, None], arrived[None], jnp.zeros_like(arrived)[None]
    )
    received = lax.all_to_all(outgoing, "dp", split_axis=0, concat_axis=0, tiled=True)
    return jnp.sum(received.astype(jnp.float32), axis=0).astype(jnp.bfloat16)


def per_device(
    segments, memory_in, seg_lengths, routes, w_query, w_key, value_weight, w_out, norm_gain
):
    rounds = segments.shape[0]
    slot_count = memory_in.shape[0]
    phase_count = lax.axis_size("phase")
    step_count = rounds * slot_count + phase_count - 1
    phase_index = lax.axis_index("phase")
    group_index = lax.axis_index("dp")
    is_first = phase_index == 0
    items = rounds * slot_count
    lengths_flat = seg_lengths.reshape(items)
    item_ids = jnp.arange(items, dtype=jnp.int32)
    mem_buf = jnp.where(is_first, memory_in[0], jnp.zeros_like(memory_in[0]))
    seg_buf = jnp.where(is_first, segments[0, 0], jnp.zeros_like(segments[0, 0]))
    mem_hist = jnp.zeros((items,) + memory_in.shape[1:], jnp.bfloat16)
    seg_hist = jnp.zeros((items,) + segments.shape[2:], jnp.bfloat16)
    for step in range(step_count):
        item_index = step - phase_index
        is_valid = (item_index >= 0) & (item_index < items)
        clipped = jnp.clip(item_index, 0, items - 1)
        length = jnp.sum(jnp.where(item_ids == clipped, lengths_flat, 0))
        mem_new, seg_new = section_layer(
            mem_buf, seg_buf, length, w_query[0], w_key[0], value_weight[0], w_out[0], norm_gain[0]
        )
        mem_current = lax.dynamic_index_in_dim(mem_hist, clipped, 0, keepdims=False)
        seg_current = lax.dynamic_index_in_dim(seg_hist, clipped, 0, keepdims=False)
        mem_hist = lax.dynamic_update_index_in_dim(
            mem_hist, jnp.where(is_valid, mem_new, mem_current), clipped, 0
        )
        seg_hist = lax.dynamic_update_index_in_dim(
            seg_hist, jnp.where(is_valid, seg_new, seg_current), clipped, 0
        )
        if step + 1 < step_count:
            mem_pass, seg_pass = shifted((mem_new, seg_new), "phase", 1)
            next_item = step + 1
            if next_item < items:
                next_round, next_slot = divmod(next_item, slot_count)
                if next_round == 0:
                    first_mem = memory_in[next_slot]
                else:
                    first_mem = route_memory(mem_pass, routes[next_slot], group_index)
                first_seg = segments[next_round, next_slot]
            else:
                first_mem = jnp.zeros_like(mem_pass)
                first_seg = jnp.zeros_like(seg_pass)
            mem_buf = jnp.where(is_first, first_mem, mem_pass)
            seg_buf = jnp.where(is_first, first_seg, seg_pass)
    mem_states = mem_hist.reshape((1, rounds, slot_count) + memory_in.shape[1:])
    seg_states = seg_hist.reshape((1, rounds, slot_count) + segments.shape[2:])
    return (mem_states, seg_states)


def solution(mesh):
    return jax.shard_map(
        per_device,
        mesh=mesh,
        in_specs=(
            P(None, "dp", "mp", None),
            P("dp", "mp", None),
            P(None, "dp"),
            P(),
            P("phase", None, "mp"),
            P("phase", None, "mp"),
            P("phase", None, "mp"),
            P("phase", "mp", None),
            P("phase", None),
        ),
        out_specs=(P("phase", None, "dp", "mp", None), P("phase", None, "dp", "mp", None)),
        check_vma=False,
    )
```

profile of v0, /device:TPU:1, one launch (start us, length us, event | category | flops | bytes accessed | tf_op | source)
XLA Modules:
  0.0 785.7 jit_solution(16878598263312502810)
XLA Ops:
  12.5 9.8 %all_gather.30 = bf16[64,4096]{1,0:T(8,128)(2,1)S(1)} all-gather(bf16[32,4096]{1,0:T(8,128)(2,1)S(1)} %get-tuple-element.64), channel_id=1, replica_groups=mesh['phase'=2,'dp'=32,'mp'=2] {'mp'}, dimensions={0}, use_global_device_ids=true | all-gather | bytes 786432 | tf_op jit(solution)/shard_map/all_gather | solution.py:28
  22.3 8.6 %all_gather.31 = bf16[64,4096]{1,0:T(8,128)(2,1)S(1)} all-gather(bf16[32,4096]{1,0:T(8,128)(2,1)S(1)} %get-tuple-element.63), channel_id=1, replica_groups=mesh['phase'=2,'dp'=32,'mp'=2] {'mp'}, dimensions={0}, use_global_device_ids=true | all-gather | bytes 786432 | tf_op jit(solution)/shard_map/all_gather | solution.py:29
  31.0 8.1 %fusion.85 = bf16[128,2048]{1,0:T(8,128)(2,1)S(1)} fusion(bf16[128,4096]{1,0:T(8,128)(2,1)S(1)} %constant_dynamic-update-slice_fusion, bf16[1,4096,2048]{2,1,0:T(8,128)(2,1)} %param.13), kind=kOutput, calls=%fused_computation.67 | convolution fusion | flops 2147745792 | bytes 18350080 | tf_op jit(solution)/shard_map/dot_general | solution.py:37
  39.5 2.9 fusion.140
  46.7 2.9 fusion.125
  51.0 8.8 %fusion.35 = bf16[2,32,4096]{2,1,0:T(8,128)(2,1)S(1)} fusion(bf16[2,32,2048]{2,1,0:T(8,128)(2,1)S(1)} %dot_general.130, bf16[1,2048,4096]{2,1,0:T(8,128)(2,1)} %param.16), kind=kOutput, calls=%fused_computation.37 | convolution fusion | flops 1074003968 | bytes 17563648 | tf_op jit(solution)/shard_map/dot_general | solution.py:67
  59.8 8.9 %fusion.38 = bf16[2,32,4096]{2,1,0:T(8,128)(2,1)S(1)} fusion(bf16[2,32,2048]{2,1,0:T(8,128)(2,1)S(1)} %dot_general.132, bf16[1,2048,4096]{2,1,0:T(8,128)(2,1)} %param.16), kind=kOutput, calls=%fused_computation.38 | convolution fusion | flops 1074003968 | bytes 17563648 | tf_op jit(solution)/shard_map/dot_general | solution.py:70
  69.8 9.5 %reduce-scatter.8.cloned.1.call-start = ((), (), s32[]{:S(2)}) async-start(), calls=%async_computation.8 | async-start | bytes 1572864 | tf_op jit(solution)/shard_map/reduce_scatter | solution.py:73
  79.3 19.4 %reduce-scatter.6.cloned.1.call-done = bf16[64,4096]{1,0:T(8,128)(2,1)} async-done(((bf16[128,4096]{1,0:T(8,128)(2,1)}), bf16[64,4096]{1,0:T(8,128)(2,1)}) %reduce-scatter.6.cloned.1.call-update) | async-done | bytes 524304 | tf_op jit(solution)/shard_map/reduce_scatter | solution.py:73
  103.5 9.7 %all_gather.32 = bf16[64,4096]{1,0:T(8,128)(2,1)S(1)} all-gather(bf16[32,4096]{1,0:T(8,128)(2,1)S(1)} %get-tuple-element.62), channel_id=1, replica_groups=mesh['phase'=2,'dp'=32,'mp'=2] {'mp'}, dimensions={0}, use_global_device_ids=true | all-gather | bytes 786432 | tf_op jit(solution)/shard_map/all_gather | solution.py:28
  113.2 8.8 %all_gather.33 = bf16[64,4096]{1,0:T(8,128)(2,1)S(1)} all-gather(bf16[32,4096]{1,0:T(8,128)(2,1)S(1)} %get-tuple-element.61), channel_id=1, replica_groups=mesh['phase'=2,'dp'=32,'mp'=2] {'mp'}, dimensions={0}, use_global_device_ids=true | all-gather | bytes 786432 | tf_op jit(solution)/shard_map/all_gather | solution.py:29
  122.1 9.1 %fusion.88 = bf16[128,2048]{1,0:T(8,128)(2,1)} fusion(bf16[128,4096]{1,0:T(8,128)(2,1)S(1)} %constant_dynamic-update-slice_fusion.2, bf16[1,4096,2048]{2,1,0:T(8,128)(2,1)} %param.13), kind=kOutput, calls=%fused_computation.68 | convolution fusion | flops 2147745792 | bytes 18350080 | tf_op jit(solution)/shard_map/dot_general | solution.py:37
  135.6 2.3 fusion.117
  140.1 2.9 fusion.128
  145.6 8.8 %fusion.41 = bf16[2,32,4096]{2,1,0:T(8,128)(2,1)S(1)} fusion(bf16[2,32,2048]{2,1,0:T(8,128)(2,1)S(1)} %dot_general.139, bf16[1,2048,4096]{2,1,0:T(8,128)(2,1)} %param.16), kind=kOutput, calls=%fused_computation.39 | convolution fusion | flops 1074003968 | bytes 17563648 | tf_op jit(solution)/shard_map/dot_general | solution.py:67
  154.8 8.8 %fusion.44 = bf16[2,32,4096]{2,1,0:T(8,128)(2,1)S(1)} fusion(bf16[2,32,2048]{2,1,0:T(8,128)(2,1)S(1)} %dot_general.141, bf16[1,2048,4096]{2,1,0:T(8,128)(2,1)} %param.16), kind=kOutput, calls=%fused_computation.40 | convolution fusion | flops 1074003968 | bytes 17563648 | tf_op jit(solution)/shard_map/dot_general | solution.py:70
  164.8 25.3 %reduce-scatter.8.cloned.1.call-done = bf16[64,4096]{1,0:T(8,128)(2,1)} async-done(((bf16[128,4096]{1,0:T(8,128)(2,1)}), bf16[64,4096]{1,0:T(8,128)(2,1)}) %reduce-scatter.8.cloned.1.call-update) | async-done | bytes 524304 | tf_op jit(solution)/shard_map/reduce_scatter | solution.py:73
  194.6 3.9 broadcast_select_fusion.1
  198.4 7.1 all-to-all-start
  208.7 122.5 %all-to-all-done = bf16[32,32,4096]{2,1,0:T(8,128)(2,1)} async-done(((bf16[32,32,4096]{2,1,0:T(8,128)(2,1)}), bf16[32,32,4096]{2,1,0:T(8,128)(2,1)}, u32[]{:S(2)}, u32[]{:S(2)}) %all-to-all-start) | async-done | bytes 8388640 | tf_op jit(solution)/shard_map/all_to_all | solution.py:93
  331.1 5.2 reduce_sum.231
  336.7 8.8 %all_gather.34 = bf16[64,4096]{1,0:T(8,128)(2,1)S(1)} all-gather(bf16[32,4096]{1,0:T(8,128)(2,1)S(1)} %get-tuple-element.60), channel_id=1, replica_groups=mesh['phase'=2,'dp'=32,'mp'=2] {'mp'}, dimensions={0}, use_global_device_ids=true | all-gather | bytes 786432 | tf_op jit(solution)/shard_map/all_gather | solution.py:28
  345.6 7.9 %all_gather.35 = bf16[64,4096]{1,0:T(8,128)(2,1)S(1)} all-gather(bf16[32,4096]{1,0:T(8,128)(2,1)S(1)} %get-tuple-element.59), channel_id=1, replica_groups=mesh['phase'=2,'dp'=32,'mp'=2] {'mp'}, dimensions={0}, use_global_device_ids=true | all-gather | bytes 786432 | tf_op jit(solution)/shard_map/all_gather | solution.py:29
  353.5 9.1 %fusion.91 = bf16[128,2048]{1,0:T(8,128)(2,1)} fusion(bf16[128,4096]{1,0:T(8,128)(2,1)S(1)} %constant_dynamic-update-slice_fusion.4, bf16[1,4096,2048]{2,1,0:T(8,128)(2,1)} %param.13), kind=kOutput, calls=%fused_computation.69 | convolution fusion | flops 2147745792 | bytes 18350080 | tf_op jit(solution)/shard_map/dot_general | solution.py:37
  367.0 2.3 fusion.115
  371.5 2.9 fusion.131
  377.0 8.8 %fusion.47 = bf16[2,32,4096]{2,1,0:T(8,128)(2,1)S(1)} fusion(bf16[2,32,2048]{2,1,0:T(8,128)(2,1)S(1)} %dot_general.148, bf16[1,2048,4096]{2,1,0:T(8,128)(2,1)} %param.16), kind=kOutput, calls=%fused_computation.41 | convolution fusion | flops 1074003968 | bytes 17563648 | tf_op jit(solution)/shard_map/dot_general | solution.py:67
  386.2 8.8 %fusion.50 = bf16[2,32,4096]{2,1,0:T(8,128)(2,1)S(1)} fusion(bf16[2,32,2048]{2,1,0:T(8,128)(2,1)S(1)} %dot_general.150, bf16[1,2048,4096]{2,1,0:T(8,128)(2,1)} %param.16), kind=kOutput, calls=%fused_computation.42 | convolution fusion | flops 1074003968 | bytes 17563648 | tf_op jit(solution)/shard_map/dot_general | solution.py:70
  396.1 42.0 %reduce-scatter.10.cloned.1.call-done = bf16[64,4096]{1,0:T(8,128)(2,1)} async-done(((bf16[128,4096]{1,0:T(8,128)(2,1)}), bf16[64,4096]{1,0:T(8,128)(2,1)}) %reduce-scatter.10.cloned.1.call-update) | async-done | bytes 524304 | tf_op jit(solution)/shard_map/reduce_scatter | solution.py:73
  441.6 3.9 broadcast_select_fusion
  445.4 7.1 all-to-all-start.1
  455.7 122.5 %all-to-all-done.1 = bf16[32,32,4096]{2,1,0:T(8,128)(2,1)} async-done(((bf16[32,32,4096]{2,1,0:T(8,128)(2,1)}), bf16[32,32,4096]{2,1,0:T(8,128)(2,1)}, u32[]{:S(2)}, u32[]{:S(2)}) %all-to-all-start.1) | async-done | bytes 8388640 | tf_op jit(solution)/shard_map/all_to_all | solution.py:93
  578.1 5.2 reduce_sum.237
  583.8 8.8 %all_gather.36 = bf16[64,4096]{1,0:T(8,128)(2,1)S(1)} all-gather(bf16[32,4096]{1,0:T(8,128)(2,1)S(1)} %get-tuple-element.58), channel_id=1, replica_groups=mesh['phase'=2,'dp'=32,'mp'=2] {'mp'}, dimensions={0}, use_global_device_ids=true | all-gather | bytes 786432 | tf_op jit(solution)/shard_map/all_gather | solution.py:28
  592.6 7.9 %all_gather.37 = bf16[64,4096]{1,0:T(8,128)(2,1)S(1)} all-gather(bf16[32,4096]{1,0:T(8,128)(2,1)S(1)} %get-tuple-element.57), channel_id=1, replica_groups=mesh['phase'=2,'dp'=32,'mp'=2] {'mp'}, dimensions={0}, use_global_device_ids=true | all-gather | bytes 786432 | tf_op jit(solution)/shard_map/all_gather | solution.py:29
  600.5 9.1 %fusion.94 = bf16[128,2048]{1,0:T(8,128)(2,1)} fusion(bf16[128,4096]{1,0:T(8,128)(2,1)S(1)} %constant_dynamic-update-slice_fusion.6, bf16[1,4096,2048]{2,1,0:T(8,128)(2,1)} %param.13), kind=kOutput, calls=%fused_computation.70 | convolution fusion | flops 2147745792 | bytes 18350080 | tf_op jit(solution)/shard_map/dot_general | solution.py:37
  614.0 2.3 fusion.113
  618.5 2.9 fusion.134
  624.0 8.8 %fusion.53 = bf16[2,32,4096]{2,1,0:T(8,128)(2,1)S(1)} fusion(bf16[2,32,2048]{2,1,0:T(8,128)(2,1)S(1)} %dot_general.157, bf16[1,2048,4096]{2,1,0:T(8,128)(2,1)} %param.16), kind=kOutput, calls=%fused_computation.43 | convolution fusion | flops 1074003968 | bytes 17563648 | tf_op jit(solution)/shard_map/dot_general | solution.py:67
  633.2 8.8 %fusion.56 = bf16[2,32,4096]{2,1,0:T(8,128)(2,1)S(1)} fusion(bf16[2,32,2048]{2,1,0:T(8,128)(2,1)S(1)} %dot_general.159, bf16[1,2048,4096]{2,1,0:T(8,128)(2,1)} %param.16), kind=kOutput, calls=%fused_computation.44 | convolution fusion | flops 1074003968 | bytes 17563648 | tf_op jit(solution)/shard_map/dot_general | solution.py:70
  643.2 41.9 %reduce-scatter.12.cloned.1.call-done = bf16[64,4096]{1,0:T(8,128)(2,1)} async-done(((bf16[128,4096]{1,0:T(8,128)(2,1)}), bf16[64,4096]{1,0:T(8,128)(2,1)}) %reduce-scatter.12.cloned.1.call-update) | async-done | bytes 524304 | tf_op jit(solution)/shard_map/reduce_scatter | solution.py:73
  689.4 9.9 %all_gather.38 = bf16[64,4096]{1,0:T(8,128)(2,1)S(1)} all-gather(bf16[32,4096]{1,0:T(8,128)(2,1)S(1)} %get-tuple-element.56), channel_id=1, replica_groups=mesh['phase'=2,'dp'=32,'mp'=2] {'mp'}, dimensions={0}, use_global_device_ids=true | all-gather | bytes 786432 | tf_op jit(solution)/shard_map/all_gather | solution.py:28
  699.3 9.0 %all_gather.39 = bf16[64,4096]{1,0:T(8,128)(2,1)S(1)} all-gather(bf16[32,4096]{1,0:T(8,128)(2,1)S(1)} %get-tuple-element.55), channel_id=1, replica_groups=mesh['phase'=2,'dp'=32,'mp'=2] {'mp'}, dimensions={0}, use_global_device_ids=true | all-gather | bytes 786432 | tf_op jit(solution)/shard_map/all_gather | solution.py:29
  708.4 9.1 %fusion.97 = bf16[128,2048]{1,0:T(8,128)(2,1)} fusion(bf16[128,4096]{1,0:T(8,128)(2,1)S(1)} %constant_dynamic-update-slice_fusion.8, bf16[1,4096,2048]{2,1,0:T(8,128)(2,1)} %param.13), kind=kOutput, calls=%fused_computation.71 | convolution fusion | flops 2147745792 | bytes 18350080 | tf_op jit(solution)/shard_map/dot_general | solution.py:37
  726.4 2.9 fusion.137
  731.9 8.8 %fusion.59 = bf16[2,32,4096]{2,1,0:T(8,128)(2,1)S(1)} fusion(bf16[2,32,2048]{2,1,0:T(8,128)(2,1)S(1)} %dot_general.166, bf16[1,2048,4096]{2,1,0:T(8,128)(2,1)} %param.16), kind=kOutput, calls=%fused_computation.45 | convolution fusion | flops 1074003968 | bytes 17563648 | tf_op jit(solution)/shard_map/dot_general | solution.py:67
  741.1 8.8 %fusion.62 = bf16[2,32,4096]{2,1,0:T(8,128)(2,1)S(1)} fusion(bf16[2,32,2048]{2,1,0:T(8,128)(2,1)S(1)} %dot_general.168, bf16[1,2048,4096]{2,1,0:T(8,128)(2,1)} %param.16), kind=kOutput, calls=%fused_computation.46 | convolution fusion | flops 1074003968 | bytes 17563648 | tf_op jit(solution)/shard_map/dot_general | solution.py:70
  751.0 25.1 %reduce-scatter.14.cloned.1.call-done = bf16[64,4096]{1,0:T(8,128)(2,1)} async-done(((bf16[128,4096]{1,0:T(8,128)(2,1)}), bf16[64,4096]{1,0:T(8,128)(2,1)}) %reduce-scatter.14.cloned.1.call-update) | async-done | bytes 524304 | tf_op jit(solution)/shard_map/reduce_scatter | solution.py:73
  (186 shorter events, 84.3 us)
Async XLA Ops:
  7.2 91.5 %reduce-scatter.6.cloned.1.call-start = ((), (), s32[]{:S(2)}) async-start(), calls=%async_computation.7 | async-start | bytes 1572864 | tf_op jit(solution)/shard_map/reduce_scatter | solution.py:73
  59.8 40.1 %copy-start.15 = (bf16[2,32,4096]{2,1,0:T(8,128)(2,1)S(1)}, bf16[2,32,4096]{2,1,0:T(8,128)(2,1)}, u32[]{:S(2)}) copy-start(bf16[2,32,4096]{2,1,0:T(8,128)(2,1)} %param.10) | copy-start | bytes 1572868
  59.8 41.1 %copy-start.12 = (bf16[2,2,32,4096]{3,2,1,0:T(8,128)(2,1)S(1)}, bf16[2,2,32,4096]{3,2,1,0:T(8,128)(2,1)}, u32[]{:S(2)}) copy-start(bf16[2,2,32,4096]{3,2,1,0:T(8,128)(2,1)} %param.9) | copy-start | bytes 3145732
  69.8 120.3 %reduce-scatter.8.cloned.1.call-start = ((), (), s32[]{:S(2)}) async-start(), calls=%async_computation.8 | async-start | bytes 1572864 | tf_op jit(solution)/shard_map/reduce_scatter | solution.py:73
  100.0 1.9 collective-permute-start
  100.9 2.1 collective-permute-start.1
  103.3 18.7 %copy-start.8 = (bf16[32,4096]{1,0:T(8,128)(2,1)}, bf16[32,4096]{1,0:T(8,128)(2,1)S(1)}, u32[]{:S(2)}) copy-start(bf16[32,4096]{1,0:T(8,128)(2,1)S(1)} %get-tuple-element.32) | copy-start | bytes 786436
  122.1 9.1 %copy-start = (bf16[1,4096,512]{2,1,0:T(8,128)(2,1)S(1)}, bf16[1,4096,512]{2,1,0:T(8,128)(2,1)}, u32[]{:S(2)}) copy-start(bf16[1,4096,512]{2,1,0:T(8,128)(2,1)} %param.14) | copy-start | bytes 12582916
  154.8 36.4 %copy-start.9 = (bf16[32,4096]{1,0:T(8,128)(2,1)S(1)}, bf16[32,4096]{1,0:T(8,128)(2,1)}, u32[]{:S(2)}) copy-start(bf16[32,4096]{1,0:T(8,128)(2,1)} %copy-done.8) | copy-start | bytes 786436
  163.6 29.6 %copy-start.17 = (s32[2,32]{1,0:T(2,128)S(1)}, s32[2,32]{1,0:T(2,128)}, u32[]{:S(2)}) copy-start(s32[2,32]{1,0:T(2,128)} %param.12) | copy-start | bytes 772
  192.1 2.5 collective-permute-start.2
  198.4 132.7 %all-to-all-start = ((bf16[32,32,4096]{2,1,0:T(8,128)(2,1)}), bf16[32,32,4096]{2,1,0:T(8,128)(2,1)}, u32[]{:S(2)}, u32[]{:S(2)}) async-start(bf16[32,32,4096]{2,1,0:T(8,128)(2,1)} %broadcast_select_fusion.1), calls=%async_computation.2 | async-start | bytes 16777216 | tf_op jit(solution)/shard_map/all_to_all | solution.py:93
  205.5 232.6 %reduce-scatter.10.cloned.1.call-start = ((), (), s32[]{:S(2)}) async-start(), calls=%async_computation.9 | async-start | bytes 1572864 | tf_op jit(solution)/shard_map/reduce_scatter | solution.py:73
  205.6 1.9 collective-permute-start.3
  336.5 16.9 %copy-start.10 = (bf16[32,4096]{1,0:T(8,128)(2,1)}, bf16[32,4096]{1,0:T(8,128)(2,1)S(1)}, u32[]{:S(2)}) copy-start(bf16[32,4096]{1,0:T(8,128)(2,1)S(1)} %get-tuple-element.28) | copy-start | bytes 786436
  353.5 9.1 %copy-start.1 = (bf16[1,4096,512]{2,1,0:T(8,128)(2,1)S(1)}, bf16[1,4096,512]{2,1,0:T(8,128)(2,1)}, u32[]{:S(2)}) copy-start(bf16[1,4096,512]{2,1,0:T(8,128)(2,1)} %param.14) | copy-start | bytes 12582916
  386.2 53.1 %copy-start.11 = (bf16[32,4096]{1,0:T(8,128)(2,1)S(1)}, bf16[32,4096]{1,0:T(8,128)(2,1)}, u32[]{:S(2)}) copy-start(bf16[32,4096]{1,0:T(8,128)(2,1)} %copy-done.10) | copy-start | bytes 786436
  439.5 2.1 collective-permute-start.4
  445.4 132.7 %all-to-all-start.1 = ((bf16[32,32,4096]{2,1,0:T(8,128)(2,1)}), bf16[32,32,4096]{2,1,0:T(8,128)(2,1)}, u32[]{:S(2)}, u32[]{:S(2)}) async-start(bf16[32,32,4096]{2,1,0:T(8,128)(2,1)} %broadcast_select_fusion), calls=%async_computation.4 | async-start | bytes 16777216 | tf_op jit(solution)/shard_map/all_to_all | solution.py:93
  452.6 232.6 %reduce-scatter.12.cloned.1.call-start = ((), (), s32[]{:S(2)}) async-start(), calls=%async_computation.10 | async-start | bytes 1572864 | tf_op jit(solution)/shard_map/reduce_scatter | solution.py:73
  452.6 1.9 collective-permute-start.5
  583.5 16.9 %copy-start.6 = (bf16[32,4096]{1,0:T(8,128)(2,1)}, bf16[32,4096]{1,0:T(8,128)(2,1)S(1)}, u32[]{:S(2)}) copy-start(bf16[32,4096]{1,0:T(8,128)(2,1)S(1)} %get-tuple-element.22) | copy-start | bytes 786436
  600.5 9.1 %copy-start.2 = (bf16[1,4096,512]{2,1,0:T(8,128)(2,1)S(1)}, bf16[1,4096,512]{2,1,0:T(8,128)(2,1)}, u32[]{:S(2)}) copy-start(bf16[1,4096,512]{2,1,0:T(8,128)(2,1)} %param.14) | copy-start | bytes 12582916
  633.2 53.1 %copy-start.7 = (bf16[32,4096]{1,0:T(8,128)(2,1)S(1)}, bf16[32,4096]{1,0:T(8,128)(2,1)}, u32[]{:S(2)}) copy-start(bf16[32,4096]{1,0:T(8,128)(2,1)} %copy-done.6) | copy-start | bytes 786436
  643.1 133.0 %reduce-scatter.14.cloned.1.call-start = ((), (), s32[]{:S(2)}) async-start(), calls=%async_computation.11 | async-start | bytes 1572864 | tf_op jit(solution)/shard_map/reduce_scatter | solution.py:73
  686.5 1.9 collective-permute-start.6
  687.2 1.7 collective-permute-start.7
  689.0 19.3 %copy-start.13 = (bf16[32,4096]{1,0:T(8,128)(2,1)}, bf16[32,4096]{1,0:T(8,128)(2,1)S(1)}, u32[]{:S(2)}) copy-start(bf16[32,4096]{1,0:T(8,128)(2,1)S(1)} %collective-permute-done.7) | copy-start | bytes 786436
  708.3 9.1 %copy-start.3 = (bf16[1,4096,512]{2,1,0:T(8,128)(2,1)S(1)}, bf16[1,4096,512]{2,1,0:T(8,128)(2,1)}, u32[]{:S(2)}) copy-start(bf16[1,4096,512]{2,1,0:T(8,128)(2,1)} %param.14) | copy-start | bytes 12582916
  708.4 13.6 %copy-start.16 = (pred[128,128]{0,1:T(8,128)(4,1)S(1)}, pred[128,128]{0,1:T(8,128)(4,1)}, u32[]{:S(2)}) copy-start(pred[128,128]{0,1:T(8,128)(4,1)} %get-tuple-element.65) | copy-start | bytes 49156
  741.0 36.2 %copy-start.14 = (bf16[32,4096]{1,0:T(8,128)(2,1)S(1)}, bf16[32,4096]{1,0:T(8,128)(2,1)}, u32[]{:S(2)}) copy-start(bf16[32,4096]{1,0:T(8,128)(2,1)} %copy-done.13) | copy-start | bytes 786436
  777.5 1.0 copy-start.4
  777.5 1.3 copy-start.5
Sparse Core Ops, SparseCore 0:
  69.9 28.7 reduce-scatter.5
  164.8 25.2 reduce-scatter.7
  396.2 41.8 reduce-scatter.9
  643.2 41.8 reduce-scatter.11
  751.1 24.9 reduce-scatter.13
where the time goes:
time: 796 us; the launch traced here: 786 us
  waiting for transfers between devices  404 us (51%)
  matrix products  183 us (23%)
  blocking collectives  89 us (11%)
  other arithmetic  46.6 us (6%)
  starting transfers between devices  29.3 us (4%)
  local copies, waits for them, and re-layouts  19.3 us (2%)
  between operations  15.1 us (2%)
    all_to_all x2, waiting for transfers between devices, route_memory(): lax.all_to_all(outgoing, 'dp', split_axis=0, concat_axis=0, tiled=True)  245 us
    reduce_scatter x5, waiting for transfers between devices, section_layer(): lax.psum_scatter(jnp.concatenate([term_mem, term_seg], axis=1).reshape(bl...  154 us
    all_gather x5, blocking collectives, section_layer(): lax.all_gather(norm_rows(mem_x, gain), 'mp', axis=0, tiled=True)  46.9 us
    dot_general x5, matrix products, section_layer(): jnp.dot(normed, w_query, preferred_element_type=jnp.float32)  44.3 us
    dot_general x5, matrix products, section_layer(): jnp.dot(attended_seg, w_out, preferred_element_type=jnp.float32)  44.2 us
    dot_general x5, matrix products, section_layer(): jnp.dot(attended_mem, w_out, preferred_element_type=jnp.float32)  44 us
    all_gather x5, blocking collectives, section_layer(): lax.all_gather(norm_rows(seg_x, gain), 'mp', axis=0, tiled=True)  42.1 us
  transfers between devices with their start and end apart: 15, of which 14 were waited for; matrix products, arithmetic and copies ran while one was open for 1% of the time, Pallas kernels for 0%

commit v1 on v0

v1 whole, which is shorter than its diff:
```python
import functools

import jax
import jax.numpy as jnp
from jax import lax
from jax.experimental import pallas as pl
from jax.experimental.pallas import tpu as pltpu
from jax.sharding import PartitionSpec as P

HEAD_SIZE = 128
EPSILON = 1e-05
CHUNKS = 4
TILE = 512
MESH = pl.DeviceIdType.MESH


def window_kernel(
    segments, memory, lengths, gain, w_query, w_key, w_value, w_out,
    mem_out, seg_out,
    wq, wk, wv, wo, gathered, rows_home, partial, received, normed, queries, keys, values, attended, far_lengths,
    wq_sem, wk_sem, wv_sem, wo_sem, len_sem, gather_send, gather_recv, home_send, home_recv, sum_send, sum_recv, out_sem,
):
    phase = lax.axis_index("phase")
    group = lax.axis_index("dp")
    half = lax.axis_index("mp")
    across = group + 1 - 2 * (group % 2)
    rounds, slots, dev_rows, width = segments.shape
    block = 2 * dev_rows
    items = rounds * slots
    chunk = width // CHUNKS
    first = phase == 0
    second = phase == 1

    def weight_copies():
        copies = []
        for tile in range(wq.shape[1] // TILE):
            cols = pl.ds(tile * TILE, TILE)
            copies.append(pltpu.make_async_copy(w_query.at[0, :, cols], wq.at[:, cols], wq_sem.at[tile]))
        copies.append(pltpu.make_async_copy(w_key.at[0], wk, wk_sem))
        copies.append(pltpu.make_async_copy(w_value.at[0], wv, wv_sem))
        for tile in range(wo.shape[1] // TILE):
            cols = pl.ds(tile * TILE, TILE)
            copies.append(pltpu.make_async_copy(w_out.at[0, :, cols], wo.at[:, cols], wo_sem.at[tile]))
        return copies

    def length_copy():
        return pltpu.make_async_remote_copy(
            src_ref=lengths, dst_ref=far_lengths, send_sem=len_sem.at[0], recv_sem=len_sem.at[1],
            device_id=(phase, across, half), device_id_type=MESH,
        )

    def input_copies(item):
        rnd, slot = item // slots, item % slots
        sources = (memory.at[slot], segments.at[rnd, slot])
        far, own = [], []
        for kind in range(2):
            for target in range(2):
                far.append(pltpu.make_async_remote_copy(
                    src_ref=sources[kind],
                    dst_ref=gathered.at[item, pl.ds(pl.multiple_of(half * block + kind * dev_rows, dev_rows), dev_rows)],
                    send_sem=gather_send.at[item, target, kind],
                    recv_sem=gather_recv.at[item, half, kind],
                    device_id=(0, across, target), device_id_type=MESH,
                ))
            own.append(pltpu.make_async_copy(
                sources[kind], rows_home.at[item, pl.ds(kind * dev_rows, dev_rows)], home_recv.at[item, kind]))
        return far, own

    def hand_copies(item, index):
        cols = pl.ds(pl.multiple_of(index * chunk, chunk), chunk)
        far = []
        for target in range(2):
            far.append(pltpu.make_async_remote_copy(
                src_ref=rows_home.at[item, :, cols],
                dst_ref=gathered.at[item, pl.ds(pl.multiple_of(half * block, block), block), cols],
                send_sem=gather_send.at[item, target, index],
                recv_sem=gather_recv.at[item, half, index],
                device_id=(1, across, target), device_id_type=MESH,
            ))
        far.append(pltpu.make_async_remote_copy(
            src_ref=rows_home.at[item, :, cols], dst_ref=rows_home.at[item, :, cols],
            send_sem=home_send.at[item, index], recv_sem=home_recv.at[item, index],
            device_id=(1, group, half), device_id_type=MESH,
        ))
        return far

    def sum_copy(item, index, target):
        cols = pl.ds(pl.multiple_of(index * chunk, chunk), chunk)
        return pltpu.make_async_remote_copy(
            src_ref=partial.at[item, pl.ds(target * block, block), cols],
            dst_ref=received.at[item, half, :, cols],
            send_sem=sum_send.at[item, index, target],
            recv_sem=sum_recv.at[item, half, index],
            device_id=(phase, across, target), device_id_type=MESH,
        )

    def out_copies(item):
        rnd, slot = item // slots, item % slots
        return (
            pltpu.make_async_copy(rows_home.at[item, pl.ds(0, dev_rows)], mem_out.at[0, rnd, slot], out_sem.at[item, 0]),
            pltpu.make_async_copy(rows_home.at[item, pl.ds(dev_rows, dev_rows)], seg_out.at[0, rnd, slot], out_sem.at[item, 1]),
        )

    barrier = pltpu.get_barrier_semaphore()
    for target in range(2):
        pl.semaphore_signal(barrier, inc=1, device_id=(phase, across, target), device_id_type=MESH)

    @pl.when(second)
    def _():
        for target in range(2):
            pl.semaphore_signal(barrier, inc=1, device_id=(0, across, target), device_id_type=MESH)
        pl.semaphore_signal(barrier, inc=1, device_id=(0, group, half), device_id_type=MESH)

    for copy in weight_copies():
        copy.start()

    @pl.when(first)
    def _():
        pl.semaphore_wait(barrier, 5)

    @pl.when(second)
    def _():
        pl.semaphore_wait(barrier, 2)

    length_copy().start()

    @pl.when(first)
    def _():
        @pl.loop(0, items)
        def _(item):
            far, own = input_copies(item)
            for copy in far + own:
                copy.start()

    length_copy().wait()

    def positions(axis):
        index = lax.broadcasted_iota(jnp.int32, (2 * block, 2 * block), axis)
        part, within = index // block, index % block
        return jnp.where(within < dev_rows, part * dev_rows + within, block + part * dev_rows + within - dev_rows)

    def compute(item):
        @pl.when(first)
        def _():
            for origin in range(2):
                for kind in range(2):
                    here = gathered.at[item, pl.ds(origin * block + kind * dev_rows, dev_rows)]
                    pltpu.make_async_copy(here, here, gather_recv.at[item, origin, kind]).wait()

        @pl.when(second)
        def _():
            for origin in range(2):
                for index in range(CHUNKS):
                    here = gathered.at[item, pl.ds(origin * block, block), pl.ds(index * chunk, chunk)]
                    pltpu.make_async_copy(here, here, gather_recv.at[item, origin, index]).wait()

        scale_row = gain[...].astype(jnp.float32)

        @pl.loop(0, 2 * block // 16)
        def _(step):
            rows = pl.ds(pl.multiple_of(step * 16, 16), 16)
            x = gathered[item, rows].astype(jnp.float32)
            scaled = x * lax.rsqrt(jnp.mean(x * x, axis=-1, keepdims=True) + EPSILON)
            normed[rows] = (scaled * scale_row).astype(jnp.bfloat16)

        @pl.loop(0, wq.shape[1] // TILE)
        def _(tile):
            cols = pl.ds(pl.multiple_of(tile * TILE, TILE), TILE)

            @pl.when(item == 0)
            def _():
                pltpu.make_async_copy(w_query.at[0, :, cols], wq.at[:, cols], wq_sem.at[tile]).wait()

            queries[:, cols] = jnp.dot(normed[...], wq[:, cols], preferred_element_type=jnp.float32).astype(jnp.bfloat16)

        @pl.when(item == 0)
        def _():
            pltpu.make_async_copy(w_key.at[0], wk, wk_sem).wait()
            pltpu.make_async_copy(w_value.at[0], wv, wv_sem).wait()

        keys[...] = jnp.dot(normed[...], wk[...], preferred_element_type=jnp.float32).astype(jnp.bfloat16)
        values[...] = jnp.dot(normed[...], wv[...], preferred_element_type=jnp.float32).astype(jnp.bfloat16)

        length = far_lengths[pl.ds(item, 1), :]
        query_pos, key_pos = positions(0), positions(1)
        visible = (key_pos < block) | (key_pos - block < length) & ((query_pos < block) | (key_pos <= query_pos))
        heads = wq.shape[1] // HEAD_SIZE
        kv_heads = wk.shape[1] // HEAD_SIZE
        per = heads // kv_heads
        for kv in range(kv_heads):
            k = keys[:, kv * HEAD_SIZE:(kv + 1) * HEAD_SIZE]
            v = values[:, kv * HEAD_SIZE:(kv + 1) * HEAD_SIZE]
            for head in range(kv * per, (kv + 1) * per):
                q = queries[:, head * HEAD_SIZE:(head + 1) * HEAD_SIZE]
                scores = lax.dot_general(q, k, (((1,), (1,)), ((), ())), preferred_element_type=jnp.float32)
                scores = jnp.where(visible, scores * HEAD_SIZE ** (-0.5), -1e30)
                weights = jnp.exp(scores - jnp.max(scores, axis=-1, keepdims=True))
                attn = (weights / jnp.sum(weights, axis=-1, keepdims=True)).astype(jnp.bfloat16)
                attended[:, head * HEAD_SIZE:(head + 1) * HEAD_SIZE] = jnp.dot(
                    attn, v, preferred_element_type=jnp.float32).astype(jnp.bfloat16)

        @pl.loop(0, CHUNKS)
        def _(index):
            for step in range(chunk // TILE):
                tile = index * (chunk // TILE) + step
                cols = pl.ds(pl.multiple_of(tile * TILE, TILE), TILE)

                @pl.when(item == 0)
                def _():
                    pltpu.make_async_copy(w_out.at[0, :, cols], wo.at[:, cols], wo_sem.at[tile]).wait()

                partial[item, :, cols] = jnp.dot(
                    attended[...], wo[:, cols], preferred_element_type=jnp.float32).astype(jnp.bfloat16)
            for target in range(2):
                sum_copy(item, index, target).start()

    def home(item):
        @pl.when(first)
        def _():
            for copy in input_copies(item)[1]:
                copy.wait()

        @pl.loop(0, CHUNKS)
        def _(index):
            cols = pl.ds(pl.multiple_of(index * chunk, chunk), chunk)

            @pl.when(second)
            def _():
                here = rows_home.at[item, :, cols]
                pltpu.make_async_copy(here, here, home_recv.at[item, index]).wait()

            for origin in range(2):
                here = received.at[item, origin, :, cols]
                pltpu.make_async_copy(here, here, sum_recv.at[item, origin, index]).wait()
            total = received[item, 0, :, cols].astype(jnp.float32) + received[item, 1, :, cols].astype(jnp.float32)
            rows_home[item, :, cols] = (rows_home[item, :, cols].astype(jnp.float32) + total).astype(jnp.bfloat16)

            @pl.when(first)
            def _():
                for copy in hand_copies(item, index):
                    copy.start()

        for copy in out_copies(item):
            copy.start()

    @pl.loop(0, items)
    def _(item):
        compute(item)

    @pl.loop(0, items)
    def _(item):
        home(item)

    @pl.loop(0, items)
    def _(item):
        for copy in out_copies(item):
            copy.wait()

        @pl.loop(0, CHUNKS)
        def _(index):
            for target in range(2):
                sum_copy(item, index, target).wait_send()

        @pl.when(first)
        def _():
            for copy in input_copies(item)[0]:
                copy.wait_send()

            @pl.loop(0, CHUNKS)
            def _(index):
                for copy in hand_copies(item, index):
                    copy.wait_send()


def run_window(segments, memory, lengths, gain, w_query, w_key, w_value, w_out):
    rounds, slots, dev_rows, width = segments.shape
    items = rounds * slots
    block = 2 * dev_rows
    rows = 2 * block
    bf16 = jnp.bfloat16
    dma = pltpu.SemaphoreType.DMA
    states = jax.ShapeDtypeStruct((1, rounds, slots, dev_rows, width), bf16)
    return pl.pallas_call(
        window_kernel,
        out_shape=(states, states),
        in_specs=[pl.BlockSpec(memory_space=pl.ANY)] * 2
        + [pl.BlockSpec(memory_space=pltpu.VMEM)] * 2
        + [pl.BlockSpec(memory_space=pl.ANY)] * 4,
        out_specs=(pl.BlockSpec(memory_space=pl.ANY), pl.BlockSpec(memory_space=pl.ANY)),
        scratch_shapes=[
            pltpu.VMEM(w_query.shape[1:], bf16),
            pltpu.VMEM(w_key.shape[1:], bf16),
            pltpu.VMEM(w_value.shape[1:], bf16),
            pltpu.VMEM(w_out.shape[1:], bf16),
            pltpu.VMEM((items, rows, width), bf16),
            pltpu.VMEM((items, block, width), bf16),
            pltpu.VMEM((items, rows, width), bf16),
            pltpu.VMEM((items, 2, block, width), bf16),
            pltpu.VMEM((rows, width), bf16),
            pltpu.VMEM((rows, w_query.shape[2]), bf16),
            pltpu.VMEM((rows, w_key.shape[2]), bf16),
            pltpu.VMEM((rows, w_value.shape[2]), bf16),
            pltpu.VMEM((rows, w_query.shape[2]), bf16),
            pltpu.VMEM(lengths.shape, jnp.int32),
            dma((w_query.shape[2] // TILE,)),
            dma,
            dma,
            dma((width // TILE,)),
            dma((2,)),
            dma((items, 2, CHUNKS)),
            dma((items, 2, CHUNKS)),
            dma((items, CHUNKS)),
            dma((items, CHUNKS)),
            dma((items, CHUNKS, 2)),
            dma((items, 2, CHUNKS)),
            dma((items, 2)),
        ],
        compiler_params=pltpu.CompilerParams(
            collective_id=0, has_side_effects=True, vmem_limit_bytes=60 * 1024 * 1024
        ),
    )(segments, memory, lengths, gain, w_query, w_key, w_value, w_out)


def route_memory(rows, routes):
    slots, dev_rows, width = rows.shape
    groups = routes.shape[1]
    pieces = jnp.moveaxis(rows.reshape(slots, dev_rows, groups, width // groups), 2, 0)
    spread = lax.all_to_all(pieces, "dp", split_axis=0, concat_axis=0, tiled=True)
    ids = jnp.arange(groups, dtype=jnp.int32)
    origin = jnp.sum(jnp.where(routes[:, None, :] == ids[None, :, None], ids[None, None, :], 0), axis=-1)
    picked = jnp.stack([jnp.take(spread[:, slot], origin[slot], axis=0) for slot in range(slots)], axis=1)
    back = lax.all_to_all(picked, "dp", split_axis=0, concat_axis=0, tiled=True)
    return jnp.moveaxis(back, 0, 2).reshape(slots, dev_rows, width)


def per_device(segments, memory_in, seg_lengths, routes, w_query, w_key, value_weight, w_out, norm_gain):
    rounds, slots = segments.shape[:2]
    memory = memory_in
    mem_states, seg_states = [], []
    for rnd in range(rounds):
        lengths = jnp.broadcast_to(jnp.pad(seg_lengths[rnd], (0, 8 - slots))[:, None], (8, 128))
        mem, seg = run_window(
            segments[rnd:rnd + 1], memory, lengths, norm_gain, w_query, w_key, value_weight, w_out)
        mem_states.append(mem)
        seg_states.append(seg)
        if rnd + 1 < rounds:
            shared = lax.ppermute(mem[0, 0], "phase", [(1, 0), (0, 1)])
            memory = route_memory(shared, routes)
    return jnp.concatenate(mem_states, axis=1), jnp.concatenate(seg_states, axis=1)


def solution(mesh):
    return jax.shard_map(
        per_device,
        mesh=mesh,
        in_specs=(
            P(None, "dp", "mp", None),
            P("dp", "mp", None),
            P(None, "dp"),
            P(),
            P("phase", None, "mp"),
            P("phase", None, "mp"),
            P("phase", None, "mp"),
            P("phase", "mp", None),
            P("phase", None),
        ),
        out_specs=(P("phase", None, "dp", "mp", None), P("phase", None, "dp", "mp", None)),
        check_vma=False,
    )
```

time: 796 us -> 224 us (0.28); the launches traced: 786 us -> 223 us
  waiting for transfers between devices: 404 us -> 24.3 us
  matrix products: 183 us -> 0 us
  Pallas kernels: 0 us -> 174 us
  blocking collectives: 89 us -> 0 us
  other arithmetic: 46.6 us -> 3.1 us
  starting transfers between devices: 29.3 us -> 12.7 us
  between operations: 15.1 us -> 0.77 us
  local copies, waits for them, and re-layouts: 19.3 us -> 8.24 us
    all_to_all x2, waiting for transfers between devices: 245 us -> 22.2 us  [the longest x1 11.4 us: route_memory(): lax.all_to_all(pieces, 'dp', split_axis=0, concat_axis=0, tiled=True)]
    pallas_call x0 -> x2, Pallas kernels: none -> 174 us  [run_window(): pl.pallas_call(window_kernel, out_shape=(states, states), in_specs=[pl.Bl...]
    dot_general x35 -> x0, matrix products: 174 us -> none  [the longest x5 44.3 us: section_layer(): jnp.dot(normed, w_query, preferred_element_type=jnp.float32)]
    reduce_scatter x5 -> x0, waiting for transfers between devices: 154 us -> none  [section_layer(): lax.psum_scatter(jnp.concatenate([term_mem, term_seg], axis=1).reshape(bl...]
    all_gather x10 -> x0, blocking collectives: 89 us -> none  [the longest x5 46.9 us: section_layer(): lax.all_gather(norm_rows(mem_x, gain), 'mp', axis=0, tiled=True)]
    reduce_sum x13 -> x1, other arithmetic: 18.2 us -> 0.11 us  [route_memory(): jnp.sum(jnp.where(routes[:, None, :] == ids[None, :, None], ids[None, Non...]
    reshape x15 -> x1, local copies, waits for them, and re-layouts: 13.1 us -> 0.86 us  [route_memory(): return jnp.moveaxis(back, 0, 2).reshape(slots, dev_rows, width)]
    reduce_scatter x5 -> x0, starting transfers between devices: 9.66 us -> none  [section_layer(): lax.psum_scatter(jnp.concatenate([term_mem, term_seg], axis=1).reshape(bl...]
  transfers between devices with their start and end apart: 15 -> 3, of which waited for: 14 -> 3; matrix products, arithmetic and copies ran while one was open for 1% -> 0% of each run, Pallas kernels for 0% -> 0%
where the time goes in v1:
time: 224 us; the launch traced here: 223 us
  Pallas kernels  174 us (78%)
  waiting for transfers between devices  24.3 us (11%)
  starting transfers between devices  12.7 us (6%)
  local copies, waits for them, and re-layouts  8.24 us (4%)
  other arithmetic  3.1 us (1%)
    pallas_call x2, Pallas kernels, run_window(): pl.pallas_call(window_kernel, out_shape=(states, states), in_specs=[pl.Bl...  174 us
    all_to_all x1, waiting for transfers between devices, route_memory(): lax.all_to_all(pieces, 'dp', split_axis=0, concat_axis=0, tiled=True)  11.4 us
    all_to_all x1, waiting for transfers between devices, route_memory(): back = lax.all_to_all(picked, 'dp', split_axis=0, concat_axis=0, tiled=True)  10.7 us
    all_to_all x1, starting transfers between devices, route_memory(): lax.all_to_all(pieces, 'dp', split_axis=0, concat_axis=0, tiled=True)  8.77 us
  transfers between devices with their start and end apart: 3, of which 3 were waited for; matrix products, arithmetic and copies ran while one was open for 0% of the time, Pallas kernels for 0%

profile of v1, /device:TPU:1, one launch (start us, length us, event | category | flops | bytes accessed | tf_op | source)
XLA Modules:
  0.0 223.5 jit_solution(17700480603623551488)
XLA Ops:
  0.6 0.8 slice_bitcast_fusion.2
  1.4 2.3 %fusion = (bf16[1,2,32,4096]{3,2,1,0:T(8,128)(2,1)}, bf16[1,2,32,4096]{3,2,1,0:T(8,128)(2,1)}) fusion(bf16[2,2,32,4096]{3,2,1,0:T(8,128)(2,1)} %param.11), kind=kLoop, calls=%fused_computation.21 | loop fusion | bytes 2097152 | tf_op jit(solution)/shard_map/slice | solution.py:343
  3.6 0.7 broadcast_in_dim.36.lengths
  4.3 0.0 copy-start.2
  4.3 86.8 %shard_map.104 = (bf16[1,1,2,32,4096]{4,3,2,1,0:T(8,128)(2,1)}, bf16[1,1,2,32,4096]{4,3,2,1,0:T(8,128)(2,1)}) custom-call(bf16[1,2,32,4096]{3,2,1,0:T(8,128)(2,1)} %get-tuple-element.15.segments, bf16[2,32,4096]{2,1,0:T(8,128)(2,1)} %memory.1, s32[8,128]{1,0:T(8,128)} %broadcast_in_dim.36.lengths, bf16[1,4096]{1,0:T(2,128)(2,1)} %gain.3, ...), custom_call_target="tpu_custom_call" | custom-call | tf_op jit(solution)/shard_map/pallas_call | solution.py:283
  91.1 0.1 collective-permute-start
  91.2 2.1 collective-permute-done
  93.3 0.9 bitcast_bitcast_fusion
  94.3 8.8 %all-to-all-start = ((bf16[32,2,32,128]{3,2,1,0:T(8,128)(2,1)}), bf16[32,2,32,128]{3,2,1,0:T(8,128)(2,1)S(1)}, u32[]{:S(2)}, u32[]{:S(2)}) async-start(bf16[32,2,32,128]{3,2,1,0:T(8,128)(2,1)} %bitcast_bitcast_fusion), calls=%async_computation | async-start | bytes 1048576 | tf_op jit(solution)/shard_map/all_to_all | solution.py:328
  103.1 0.0 copy-done.2
  103.1 0.1 select_reduce_fusion
  103.2 11.4 %all-to-all-done = bf16[32,2,32,128]{3,2,1,0:T(8,128)(2,1)S(1)} async-done(((bf16[32,2,32,128]{3,2,1,0:T(8,128)(2,1)}), bf16[32,2,32,128]{3,2,1,0:T(8,128)(2,1)S(1)}, u32[]{:S(2)}, u32[]{:S(2)}) %all-to-all-start) | async-done | bytes 524320 | tf_op jit(solution)/shard_map/all_to_all | solution.py:328
  114.7 0.6 gather_fusion
  115.3 0.1 select_bitcast_fusion.1
  115.4 0.6 gather_fusion.1
  116.0 0.1 select_bitcast_fusion
  116.1 0.1 pad_maximum_fusion.2
  116.2 0.9 copy.21
  117.0 3.9 %all-to-all-start.1 = ((bf16[32,2,32,128]{3,2,1,0:T(8,128)(2,1)}), bf16[32,2,32,128]{3,2,1,0:T(8,128)(2,1)S(1)}, u32[]{:S(2)}, u32[]{:S(2)}) async-start(bf16[32,2,32,128]{3,2,1,0:T(8,128)(2,1)} %copy.21), calls=%async_computation.1 | async-start | bytes 1048576 | tf_op jit(solution)/shard_map/all_to_all | solution.py:332
  121.0 10.7 %all-to-all-done.1 = bf16[32,2,32,128]{3,2,1,0:T(8,128)(2,1)S(1)} async-done(((bf16[32,2,32,128]{3,2,1,0:T(8,128)(2,1)}), bf16[32,2,32,128]{3,2,1,0:T(8,128)(2,1)S(1)}, u32[]{:S(2)}, u32[]{:S(2)}) %all-to-all-start.1) | async-done | bytes 524320 | tf_op jit(solution)/shard_map/all_to_all | solution.py:332
  131.7 0.9 copy_bitcast_fusion.memory
  132.6 0.7 broadcast_in_dim.39.lengths
  133.2 0.0 copy-start
  133.2 0.0 copy-start.1
  133.2 87.5 %shard_map.105 = (bf16[1,1,2,32,4096]{4,3,2,1,0:T(8,128)(2,1)}, bf16[1,1,2,32,4096]{4,3,2,1,0:T(8,128)(2,1)}) custom-call(bf16[1,2,32,4096]{3,2,1,0:T(8,128)(2,1)} %get-tuple-element.16.segments, bf16[2,32,4096]{2,1,0:T(8,128)(2,1)} %copy_bitcast_fusion.memory, s32[8,128]{1,0:T(8,128)} %broadcast_in_dim.39.lengths, bf16[1,4096]{1,0:T(2,128)(2,1)} %gain.3, ...), custom_call_target="tpu_custom_call" | custom-call | tf_op jit(solution)/shard_map/pallas_call | solution.py:283
  220.8 0.0 copy-done
  220.8 0.0 copy-done.1
  220.8 2.7 %pad_maximum_fusion = (bf16[1,2,2,32,4096]{4,3,2,1,0:T(8,128)(2,1)}, bf16[1,2,2,32,4096]{4,3,2,1,0:T(8,128)(2,1)}) fusion(bf16[1,1,2,32,4096]{4,3,2,1,0:T(8,128)(2,1)} %get-tuple-element.8, bf16[1,1,2,32,4096]{4,3,2,1,0:T(8,128)(2,1)S(1)} %copy-done, bf16[1,1,2,32,4096]{4,3,2,1,0:T(8,128)(2,1)} %get-tuple-element.10, bf16[1,1,2,32,4096]{4,3,2,1,0:T(8,128)(2,1)S(1)} %copy-done.1), kind=kLoop, calls=%fused_computation.2 | loop fusion | flops 1048576 | bytes 4194304 | tf_op jit(solution)/shard_map/concatenate | solution.py:349
  (6 shorter events, 0.1 us)
Async XLA Ops:
  4.3 98.7 %copy-start.2 = (s32[2,32]{1,0:T(2,128)S(1)}, s32[2,32]{1,0:T(2,128)}, u32[]{:S(2)}) copy-start(s32[2,32]{1,0:T(2,128)} %param.14) | copy-start | bytes 772
  91.1 2.2 collective-permute-start
  94.3 20.4 %all-to-all-start = ((bf16[32,2,32,128]{3,2,1,0:T(8,128)(2,1)}), bf16[32,2,32,128]{3,2,1,0:T(8,128)(2,1)S(1)}, u32[]{:S(2)}, u32[]{:S(2)}) async-start(bf16[32,2,32,128]{3,2,1,0:T(8,128)(2,1)} %bitcast_bitcast_fusion), calls=%async_computation | async-start | bytes 1048576 | tf_op jit(solution)/shard_map/all_to_all | solution.py:328
  117.0 14.7 %all-to-all-start.1 = ((bf16[32,2,32,128]{3,2,1,0:T(8,128)(2,1)}), bf16[32,2,32,128]{3,2,1,0:T(8,128)(2,1)S(1)}, u32[]{:S(2)}, u32[]{:S(2)}) async-start(bf16[32,2,32,128]{3,2,1,0:T(8,128)(2,1)} %copy.21), calls=%async_computation.1 | async-start | bytes 1048576 | tf_op jit(solution)/shard_map/all_to_all | solution.py:332
  133.2 87.6 %copy-start = (bf16[1,1,2,32,4096]{4,3,2,1,0:T(8,128)(2,1)S(1)}, bf16[1,1,2,32,4096]{4,3,2,1,0:T(8,128)(2,1)}, u32[]{:S(2)}) copy-start(bf16[1,1,2,32,4096]{4,3,2,1,0:T(8,128)(2,1)} %get-tuple-element.7) | copy-start | bytes 1572868
  133.2 87.6 %copy-start.1 = (bf16[1,1,2,32,4096]{4,3,2,1,0:T(8,128)(2,1)S(1)}, bf16[1,1,2,32,4096]{4,3,2,1,0:T(8,128)(2,1)}, u32[]{:S(2)}) copy-start(bf16[1,1,2,32,4096]{4,3,2,1,0:T(8,128)(2,1)} %get-tuple-element.9) | copy-start | bytes 1572868

commit v2 on v1

--- a/solution.py
+++ b/solution.py
@@ -10,19 +10,23 @@
 HEAD_SIZE = 128
 EPSILON = 1e-05
 CHUNKS = 4
-TILE = 512
+TILE = 1024
+PIECE = 128
 MESH = pl.DeviceIdType.MESH
 
 
 def window_kernel(
-    segments, memory, lengths, gain, w_query, w_key, w_value, w_out,
+    segments, memory, lengths, origins, gain, w_query, w_key, w_value, w_out,
     mem_out, seg_out,
-    wq, wk, wv, wo, gathered, rows_home, partial, received, normed, queries, keys, values, attended, far_lengths,
+    wq, wk, wv, wo, gathered, rows_home, partial, received, normed, queries, keys, values, attended, far_lengths, spread_even, spread_odd, picked,
     wq_sem, wk_sem, wv_sem, wo_sem, len_sem, gather_send, gather_recv, home_send, home_recv, sum_send, sum_recv, out_sem,
+    route_send, route_recv, back_send, back_recv,
 ):
     phase = lax.axis_index("phase")
     group = lax.axis_index("dp")
     half = lax.axis_index("mp")
+    groups = lax.axis_size("dp")
+    spread = (spread_even, spread_odd)
     across = group + 1 - 2 * (group % 2)
     rounds, slots, dev_rows, width = segments.shape
     block = 2 * dev_rows
@@ -49,22 +53,66 @@
             device_id=(phase, across, half), device_id_type=MESH,
         )
 
-    def input_copies(item):
-        rnd, slot = item // slots, item % slots
-        sources = (memory.at[slot], segments.at[rnd, slot])
-        far, own = [], []
-        for kind in range(2):
-            for target in range(2):
-                far.append(pltpu.make_async_remote_copy(
-                    src_ref=sources[kind],
-                    dst_ref=gathered.at[item, pl.ds(pl.multiple_of(half * block + kind * dev_rows, dev_rows), dev_rows)],
-                    send_sem=gather_send.at[item, target, kind],
-                    recv_sem=gather_recv.at[item, half, kind],
-                    device_id=(0, across, target), device_id_type=MESH,
-                ))
-            own.append(pltpu.make_async_copy(
-                sources[kind], rows_home.at[item, pl.ds(kind * dev_rows, dev_rows)], home_recv.at[item, kind]))
-        return far, own
+    def row_copies(item, source, kind):
+        return [
+            pltpu.make_async_remote_copy(
+                src_ref=source,
+                dst_ref=gathered.at[item, pl.ds(pl.multiple_of(half * block + kind * dev_rows, dev_rows), dev_rows)],
+                send_sem=gather_send.at[item, target, kind],
+                recv_sem=gather_recv.at[item, half, kind],
+                device_id=(0, across, target), device_id_type=MESH,
+            )
+            for target in range(2)
+        ]
+
+    def memory_copies(item):
+        return row_copies(item, memory.at[item], 0)
+
+    def segment_copies(item):
+        return row_copies(item, segments.at[item // slots, item % slots], 1)
+
+    def routed_copies(item):
+        return row_copies(item, rows_home.at[item, pl.ds(0, dev_rows)], 0)
+
+    def own_memory(item):
+        return pltpu.make_async_copy(memory.at[item], rows_home.at[item, pl.ds(0, dev_rows)], home_recv.at[item, 0])
+
+    def own_segment(item):
+        return pltpu.make_async_copy(
+            segments.at[item // slots, item % slots], rows_home.at[item, pl.ds(dev_rows, dev_rows)], home_recv.at[item, 1])
+
+    def piece_copy(slot, piece):
+        return pltpu.make_async_remote_copy(
+            src_ref=rows_home.at[slot, pl.ds(0, dev_rows), pl.ds(pl.multiple_of(piece * PIECE, PIECE), PIECE)],
+            dst_ref=spread[slot].at[group],
+            send_sem=route_send.at[slot], recv_sem=route_recv.at[slot],
+            device_id=(0, piece, half), device_id_type=MESH,
+        )
+
+    own_piece = pl.ds(pl.multiple_of(group * PIECE, PIECE), PIECE)
+
+    def middle(slot):
+        pltpu.make_async_copy(spread[slot], spread[slot], route_recv.at[slot]).wait()
+        item = slots + slot
+        rows_home[item, pl.ds(0, dev_rows), own_piece] = spread[slot][origins[slot, group]]
+
+        @pl.loop(1, groups)
+        def _(step):
+            target = (group + step) % groups
+            picked[slot, target] = spread[slot][origins[slot, target]]
+            pltpu.make_async_remote_copy(
+                src_ref=picked.at[slot, target],
+                dst_ref=rows_home.at[item, pl.ds(0, dev_rows), own_piece],
+                send_sem=back_send.at[slot], recv_sem=back_recv.at[slot],
+                device_id=(0, target, half), device_id_type=MESH,
+            ).start()
+
+    def forward(slot):
+        item = slots + slot
+        here = picked.at[slot, pl.ds(0, groups - 1)]
+        pltpu.make_async_copy(here, here, back_recv.at[slot]).wait()
+        for copy in routed_copies(item):
+            copy.start()
 
     def hand_copies(item, index):
         cols = pl.ds(pl.multiple_of(index * chunk, chunk), chunk)
@@ -116,21 +164,33 @@
 
     @pl.when(first)
     def _():
-        pl.semaphore_wait(barrier, 5)
+        @pl.loop(0, groups)
+        def _(target):
+            pl.semaphore_signal(barrier, inc=1, device_id=(1, target, half), device_id_type=MESH)
+
+        @pl.loop(1, groups)
+        def _(step):
+            pl.semaphore_signal(barrier, inc=1, device_id=(0, (group + step) % groups, half), device_id_type=MESH)
+
+        pl.semaphore_wait(barrier, 5 + groups - 1)
 
     @pl.when(second)
     def _():
-        pl.semaphore_wait(barrier, 2)
+        pl.semaphore_wait(barrier, 2 + groups)
 
     length_copy().start()
 
     @pl.when(first)
     def _():
+        @pl.loop(0, slots)
+        def _(item):
+            for copy in memory_copies(item) + segment_copies(item):
+                copy.start()
+            own_memory(item).start()
+
         @pl.loop(0, items)
         def _(item):
-            far, own = input_copies(item)
-            for copy in far + own:
-                copy.start()
+            own_segment(item).start()
 
     length_copy().wait()
 
@@ -139,7 +199,7 @@
         part, within = index // block, index % block
         return jnp.where(within < dev_rows, part * dev_rows + within, block + part * dev_rows + within - dev_rows)
 
-    def compute(item):
+    def project(item):
         @pl.when(first)
         def _():
             for origin in range(2):
@@ -173,6 +233,7 @@
 
             queries[:, cols] = jnp.dot(normed[...], wq[:, cols], preferred_element_type=jnp.float32).astype(jnp.bfloat16)
 
+    def attend(item):
         @pl.when(item == 0)
         def _():
             pltpu.make_async_copy(w_key.at[0], wk, wk_sem).wait()
@@ -187,17 +248,20 @@
         heads = wq.shape[1] // HEAD_SIZE
         kv_heads = wk.shape[1] // HEAD_SIZE
         per = heads // kv_heads
+        seen = jnp.concatenate([visible] * per, axis=0)
         for kv in range(kv_heads):
             k = keys[:, kv * HEAD_SIZE:(kv + 1) * HEAD_SIZE]
             v = values[:, kv * HEAD_SIZE:(kv + 1) * HEAD_SIZE]
-            for head in range(kv * per, (kv + 1) * per):
-                q = queries[:, head * HEAD_SIZE:(head + 1) * HEAD_SIZE]
-                scores = lax.dot_general(q, k, (((1,), (1,)), ((), ())), preferred_element_type=jnp.float32)
-                scores = jnp.where(visible, scores * HEAD_SIZE ** (-0.5), -1e30)
-                weights = jnp.exp(scores - jnp.max(scores, axis=-1, keepdims=True))
-                attn = (weights / jnp.sum(weights, axis=-1, keepdims=True)).astype(jnp.bfloat16)
-                attended[:, head * HEAD_SIZE:(head + 1) * HEAD_SIZE] = jnp.dot(
-                    attn, v, preferred_element_type=jnp.float32).astype(jnp.bfloat16)
+            q = jnp.concatenate(
+                [queries[:, head * HEAD_SIZE:(head + 1) * HEAD_SIZE] for head in range(kv * per, (kv + 1) * per)], axis=0)
+            scores = lax.dot_general(q, k, (((1,), (1,)), ((), ())), preferred_element_type=jnp.float32)
+            scores = jnp.where(seen, scores * HEAD_SIZE ** (-0.5), -1e30)
+            weights = jnp.exp(scores - jnp.max(scores, axis=-1, keepdims=True))
+            attn = (weights * (1.0 / jnp.sum(weights, axis=-1, keepdims=True))).astype(jnp.bfloat16)
+            mixed = jnp.dot(attn, v, preferred_element_type=jnp.float32).astype(jnp.bfloat16)
+            for step in range(per):
+                head = kv * per + step
+                attended[:, head * HEAD_SIZE:(head + 1) * HEAD_SIZE] = mixed[step * 2 * block:(step + 1) * 2 * block]
 
         @pl.loop(0, CHUNKS)
         def _(index):
@@ -214,11 +278,19 @@
             for target in range(2):
                 sum_copy(item, index, target).start()
 
-    def home(item):
+    def home(item, slot):
         @pl.when(first)
         def _():
-            for copy in input_copies(item)[1]:
-                copy.wait()
+            own_segment(item).wait()
+
+            @pl.when(item < slots)
+            def _():
+                own_memory(slot).wait()
+
+            @pl.when(item >= slots)
+            def _():
+                for copy in routed_copies(item):
+                    copy.wait_send()
 
         @pl.loop(0, CHUNKS)
         def _(index):
@@ -240,16 +312,50 @@
                 for copy in hand_copies(item, index):
                     copy.start()
 
+            @pl.when(second & (item < slots))
+            def _():
+                @pl.loop(0, groups // CHUNKS)
+                def _(step):
+                    piece_copy(slot, index * (groups // CHUNKS) + step).start()
+
         for copy in out_copies(item):
             copy.start()
 
     @pl.loop(0, items)
     def _(item):
-        compute(item)
-
-    @pl.loop(0, items)
-    def _(item):
-        home(item)
+        later = first & (item == slots)
+
+        @pl.when(later)
+        def _():
+            middle(0)
+            forward(0)
+
+        project(item)
+
+        @pl.when(item % 2 == 1)
+        def _():
+            home(item - 1, 0)
+
+        @pl.when(first & (item == 0))
+        def _():
+            @pl.loop(slots, items)
+            def _(other):
+                for copy in segment_copies(other):
+                    copy.start()
+
+        @pl.when(later)
+        def _():
+            middle(1)
+
+        attend(item)
+
+        @pl.when(later)
+        def _():
+            forward(1)
+
+        @pl.when(item % 2 == 1)
+        def _():
+            home(item, 1)
 
     @pl.loop(0, items)
     def _(item):
@@ -263,7 +369,7 @@
 
         @pl.when(first)
         def _():
-            for copy in input_copies(item)[0]:
+            for copy in segment_copies(item):
                 copy.wait_send()
 
             @pl.loop(0, CHUNKS)
@@ -271,8 +377,20 @@
                 for copy in hand_copies(item, index):
                     copy.wait_send()
 
-
-def run_window(segments, memory, lengths, gain, w_query, w_key, w_value, w_out):
+    for slot in range(slots):
+        @pl.when(first)
+        def _():
+            for copy in memory_copies(slot):
+                copy.wait_send()
+            here = picked.at[slot, pl.ds(0, groups - 1)]
+            pltpu.make_async_copy(here, here, back_send.at[slot]).wait()
+
+        @pl.when(second)
+        def _():
+            pltpu.make_async_copy(spread[slot], spread[slot], route_send.at[slot]).wait()
+
+
+def run_window(segments, memory, lengths, origins, gain, w_query, w_key, w_value, w_out):
     rounds, slots, dev_rows, width = segments.shape
     items = rounds * slots
     block = 2 * dev_rows
@@ -284,7 +402,7 @@
         window_kernel,
         out_shape=(states, states),
         in_specs=[pl.BlockSpec(memory_space=pl.ANY)] * 2
-        + [pl.BlockSpec(memory_space=pltpu.VMEM)] * 2
+        + [pl.BlockSpec(memory_space=pltpu.VMEM), pl.BlockSpec(memory_space=pltpu.SMEM), pl.BlockSpec(memory_space=pltpu.VMEM)]
         + [pl.BlockSpec(memory_space=pl.ANY)] * 4,
         out_specs=(pl.BlockSpec(memory_space=pl.ANY), pl.BlockSpec(memory_space=pl.ANY)),
         scratch_shapes=[
@@ -302,6 +420,9 @@
             pltpu.VMEM((rows, w_value.shape[2]), bf16),
             pltpu.VMEM((rows, w_query.shape[2]), bf16),
             pltpu.VMEM(lengths.shape, jnp.int32),
+            pltpu.VMEM((width // PIECE, dev_rows, PIECE), bf16),
+            pltpu.VMEM((width // PIECE, dev_rows, PIECE), bf16),
+            pltpu.VMEM((slots, width // PIECE, dev_rows, PIECE), bf16),
             dma((w_query.shape[2] // TILE,)),
             dma,
             dma,
@@ -314,39 +435,24 @@
             dma((items, CHUNKS, 2)),
             dma((items, 2, CHUNKS)),
             dma((items, 2)),
+            dma((slots,)),
+            dma((slots,)),
+            dma((slots,)),
+            dma((slots,)),
         ],
         compiler_params=pltpu.CompilerParams(
-            collective_id=0, has_side_effects=True, vmem_limit_bytes=60 * 1024 * 1024
+            collective_id=0, has_side_effects=True, vmem_limit_bytes=62 * 1024 * 1024
         ),
-    )(segments, memory, lengths, gain, w_query, w_key, w_value, w_out)
-
-
-def route_memory(rows, routes):
-    slots, dev_rows, width = rows.shape
+    )(segments, memory, lengths, origins, gain, w_query, w_key, w_value, w_out)
+
+
+def per_device(segments, memory_in, seg_lengths, routes, w_query, w_key, value_weight, w_out, norm_gain):
     groups = routes.shape[1]
-    pieces = jnp.moveaxis(rows.reshape(slots, dev_rows, groups, width // groups), 2, 0)
-    spread = lax.all_to_all(pieces, "dp", split_axis=0, concat_axis=0, tiled=True)
+    lengths = jnp.broadcast_to(jnp.pad(seg_lengths.reshape(-1), (0, 8 - seg_lengths.size))[:, None], (8, 128))
     ids = jnp.arange(groups, dtype=jnp.int32)
-    origin = jnp.sum(jnp.where(routes[:, None, :] == ids[None, :, None], ids[None, None, :], 0), axis=-1)
-    picked = jnp.stack([jnp.take(spread[:, slot], origin[slot], axis=0) for slot in range(slots)], axis=1)
-    back = lax.all_to_all(picked, "dp", split_axis=0, concat_axis=0, tiled=True)
-    return jnp.moveaxis(back, 0, 2).reshape(slots, dev_rows, width)
-
-
-def per_device(segments, memory_in, seg_lengths, routes, w_query, w_key, value_weight, w_out, norm_gain):
-    rounds, slots = segments.shape[:2]
-    memory = memory_in
-    mem_states, seg_states = [], []
-    for rnd in range(rounds):
-        lengths = jnp.broadcast_to(jnp.pad(seg_lengths[rnd], (0, 8 - slots))[:, None], (8, 128))
-        mem, seg = run_window(
-            segments[rnd:rnd + 1], memory, lengths, norm_gain, w_query, w_key, value_weight, w_out)
-        mem_states.append(mem)
-        seg_states.append(seg)
-        if rnd + 1 < rounds:
-            shared = lax.ppermute(mem[0, 0], "phase", [(1, 0), (0, 1)])
-            memory = route_memory(shared, routes)
-    return jnp.concatenate(mem_states, axis=1), jnp.concatenate(seg_states, axis=1)
+    origins = jnp.sum(jnp.where(routes[:, None, :] == ids[None, :, None], ids[None, None, :], 0), axis=-1)
+    return run_window(
+        segments, memory_in, lengths, origins, norm_gain, w_query, w_key, value_weight, w_out)
 
 
 def solution(mesh):

time: 224 us -> 149 us (0.67)
  Pallas kernels: 174 us -> 141 us
  waiting for transfers between devices: 24.3 us -> 0 us
  starting transfers between devices: 12.7 us -> 0 us
  local copies, waits for them, and re-layouts: 8.24 us -> 6 us
    pallas_call x2 -> x1, Pallas kernels: 174 us -> 141 us  [run_window(): pl.pallas_call(window_kernel, out_shape=(states, states), in_specs=[pl.Bl...]
    all_to_all x2 -> x0, waiting for transfers between devices: 22.2 us -> none  [the longest x1 11.4 us: route_memory(): lax.all_to_all(pieces, 'dp', split_axis=0, concat_axis=0, tiled=True)]
    all_to_all x2 -> x0, starting transfers between devices: 12.7 us -> none  [the longest x1 8.77 us: route_memory(): lax.all_to_all(pieces, 'dp', split_axis=0, concat_axis=0, tiled=True)]
    unnamed x6 -> x2, local copies, waits for them, and re-layouts: 0.01 us -> 4.57 us
    concatenate x1 -> x0, other arithmetic: 2.71 us -> none  [per_device(): jnp.concatenate(mem_states, axis=1)]
    slice x1 -> x0, local copies, waits for them, and re-layouts: 2.26 us -> none  [per_device(): segments[rnd:rnd + 1]]
  transfers between devices with their start and end apart: 3 -> 0, of which waited for: 3 -> 0; matrix products, arithmetic and copies ran while one was open for 0% -> 0% of each run, Pallas kernels for 0% -> 0%
where the time goes in v2:
time: 149 us
  Pallas kernels  141 us (95%)
  local copies, waits for them, and re-layouts  6 us (4%)
    pallas_call x1, Pallas kernels, run_window(): pl.pallas_call(window_kernel, out_shape=(states, states), in_specs=[pl.Bl...  141 us
    unnamed x2, local copies, waits for them, and re-layouts  4.57 us

profile of v2, /device:TPU:1, one launch (start us, length us, event | category | flops | bytes accessed | tf_op | source)
XLA Modules:
  0.0 149.0 jit_solution(14512133786388303533)
XLA Ops:
  0.6 0.8 reshape.9
  1.4 1.4 select_reduce_fusion.origins
  2.8 0.7 broadcast_in_dim.10.lengths
  3.4 141.0 %shard_map.104 = (bf16[1,2,2,32,4096]{4,3,2,1,0:T(8,128)(2,1)}, bf16[1,2,2,32,4096]{4,3,2,1,0:T(8,128)(2,1)}) custom-call(bf16[2,2,32,4096]{3,2,1,0:T(8,128)(2,1)} %segments.1, bf16[2,32,4096]{2,1,0:T(8,128)(2,1)} %memory.1, s32[8,128]{1,0:T(8,128)} %broadcast_in_dim.10.lengths, s32[2,32]{1,0:T(2,128)} %select_reduce_fusion.origins, bf16[1,4096]{1,0:T(2,128)(2,1)} %gain.1, ...), custom_call_target="tpu_custom_call" | custom-call | tf_op jit(solution)/shard_map/pallas_call | solution.py:401
  144.4 2.3 %copy.13 = bf16[1,2,2,32,4096]{4,3,2,1,0:T(8,128)(2,1)} copy(bf16[1,2,2,32,4096]{4,3,2,1,0:T(8,128)(2,1)} %get-tuple-element.4) | data formatting | bytes 2097152
  146.7 2.3 %copy.14 = bf16[1,2,2,32,4096]{4,3,2,1,0:T(8,128)(2,1)} copy(bf16[1,2,2,32,4096]{4,3,2,1,0:T(8,128)(2,1)} %get-tuple-element.5) | data formatting | bytes 2097152
  (1 shorter events, 0.0 us)

commit v3 on v0

v3 whole, which is shorter than its diff:
```python
import jax
import jax.numpy as jnp
from jax import lax
from jax.experimental import pallas as pl
from jax.experimental.pallas import tpu as pltpu
from jax.sharding import PartitionSpec as P

HEAD_SIZE = 128
EPSILON = 1e-05
CHUNKS = 4
AHEAD = 4
PIECE = 128
BAND = 32
MESH = pl.DeviceIdType.MESH
F32 = jnp.float32
BF16 = jnp.bfloat16


def window_kernel(
    segments, memory, lengths, routes, gain, w_query, w_key, w_value, w_out,
    mem_out, seg_out,
    wq, wk, wv, wo, rows_in, partial, own_sum, far_sum, last_sum, scaled, squares, acc_q, acc_k, acc_v,
    queries, keys, values, attended, spread_even, spread_odd, picked, origins,
    win_sem, wo_sem, own_sem, gather_send, gather_recv, keep_send, keep_recv, far_send, far_recv, near_send, near_recv,
    mem_send, mem_recv, seg_send, seg_recv, state_send, state_recv, out_sem, route_send, route_recv, back_send, back_recv, known_sem,
):
    phase = lax.axis_index("phase")
    group = lax.axis_index("dp")
    half = lax.axis_index("mp")
    groups = lax.axis_size("dp")
    peer = 1 - half
    rounds, slots, dev_rows, width = segments.shape
    mem_rows = 2 * dev_rows
    rows = 2 * mem_rows
    items = rounds * slots
    chunk = width // CHUNKS
    first = phase == 0
    second = phase == 1
    spread = (spread_even, spread_odd)
    mem_home = pl.multiple_of(half * dev_rows, dev_rows)
    seg_home = pl.multiple_of(mem_rows + half * dev_rows, dev_rows)
    mem_peer = pl.multiple_of(peer * dev_rows, dev_rows)
    seg_peer = pl.multiple_of(mem_rows + peer * dev_rows, dev_rows)

    def columns(index):
        return pl.ds(pl.multiple_of(index * chunk, chunk), chunk)

    def arrived(ref, sem):
        pltpu.make_async_copy(ref, ref, sem).wait()

    def remote(source, target, send, recv, device):
        return pltpu.make_async_remote_copy(
            src_ref=source, dst_ref=target, send_sem=send, recv_sem=recv, device_id=device, device_id_type=MESH)

    def in_copies(index):
        depth = pl.ds(index * chunk, chunk)
        return [
            pltpu.make_async_copy(source.at[0, depth], target.at[depth], win_sem.at[index, which])
            for which, (source, target) in enumerate(((w_query, wq), (w_key, wk), (w_value, wv)))
        ]

    def wo_copy(index):
        cols = columns(index)
        return pltpu.make_async_copy(w_out.at[0, :, cols], wo.at[:, cols], wo_sem.at[index])

    def entry_source(item, kind):
        return memory.at[item] if kind == 0 else segments.at[item // slots, item % slots]

    def entry_own(item, kind):
        return pltpu.make_async_copy(
            entry_source(item, kind), rows_in.at[item, pl.ds((mem_home, seg_home)[kind], dev_rows)], own_sem.at[item, kind])

    def entry_far(item, kind, index):
        cols = pl.ds(index * chunk, chunk)
        return remote(entry_source(item, kind).at[:, cols],
                      rows_in.at[item, pl.ds((mem_home, seg_home)[kind], dev_rows), cols],
                      gather_send.at[item, kind, index], gather_recv.at[item, kind, index], (0, group, peer))

    def entry_wait(item, kind, index):
        cols = pl.ds(index * chunk, chunk)
        arrived(rows_in.at[item, pl.ds((mem_peer, seg_peer)[kind], dev_rows), cols], gather_recv.at[item, kind, index])

    def keep_copy(item):
        return remote(rows_in.at[item], rows_in.at[item], keep_send.at[item], keep_recv.at[item], (1, group, half))

    def far_copy(item, index):
        slot, cols = item % slots, columns(index)
        return remote(partial.at[slot, :, cols], far_sum.at[slot, :, cols], far_send.at[item, index],
                      far_recv.at[item, index], (1, group, peer))

    def near_copy(item, index):
        slot, cols = item % slots, columns(index)
        return remote(partial.at[slot, :, cols], own_sum.at[slot, :, cols], near_send.at[item, index],
                      near_recv.at[item, index], (1, group, half))

    def mem_all(item, index):
        slot, cols = item % slots, columns(index)
        span = pl.ds(0, mem_rows)
        return remote(partial.at[slot, span, cols], last_sum.at[item, span, cols], mem_send.at[item, index],
                      mem_recv.at[item, index], (1, group, peer))

    def mem_part(item, index):
        slot, cols = item % slots, columns(index)
        return remote(partial.at[slot, pl.ds(mem_peer, dev_rows), cols], last_sum.at[item, pl.ds(0, dev_rows), cols],
                      mem_send.at[item, index], mem_recv.at[item, index], (1, group, peer))

    def seg_part(item):
        slot = item % slots
        return remote(partial.at[slot, pl.ds(seg_peer, dev_rows)], last_sum.at[item, pl.ds(mem_rows, dev_rows)],
                      seg_send.at[item], seg_recv.at[item], (1, group, peer))

    def states(item):
        rnd, slot = item // slots, item % slots
        return ((rows_in.at[item, pl.ds(mem_home, dev_rows)], mem_out.at[0, rnd, slot]),
                (rows_in.at[item, pl.ds(seg_home, dev_rows)], seg_out.at[0, rnd, slot]))

    def state_copies(item):
        return [remote(source, target, state_send.at[item, kind], state_recv.at[item, kind], (0, group, half))
                for kind, (source, target) in enumerate(states(item))]

    def out_copy(item, kind):
        source, target = states(item)[kind]
        return pltpu.make_async_copy(source, target, out_sem.at[item, kind])

    own_piece = pl.ds(pl.multiple_of(group * PIECE, PIECE), PIECE)

    def piece_copy(slot, piece):
        return remote(rows_in.at[slot, pl.ds(0, mem_rows), pl.ds(pl.multiple_of(piece * PIECE, PIECE), PIECE)],
                      spread[slot].at[group], route_send.at[slot], route_recv.at[slot], (0, piece, half))

    def reorder(slot):
        item = slots + slot
        arrived(spread[slot], route_recv.at[slot])
        for index in range(CHUNKS):
            entry_far(item, 1, index).start()
        rows_in[item, pl.ds(0, mem_rows), own_piece] = spread[slot][origins[slot, group]]

        @pl.loop(1, groups)
        def _(step):
            target = (group + step) % groups
            picked[slot, target] = spread[slot][origins[slot, target]]
            remote(picked.at[slot, target], rows_in.at[item, pl.ds(0, mem_rows), own_piece],
                   back_send.at[slot], back_recv.at[slot], (0, target, half)).start()

        arrived(picked.at[slot, pl.ds(0, groups - 1)], back_recv.at[slot])

    barrier = pltpu.get_barrier_semaphore()

    def greet(device):
        pl.semaphore_signal(barrier, inc=1, device_id=device, device_id_type=MESH)

    greet((phase, group, peer))

    @pl.when(second)
    def _():
        greet((0, group, half))
        greet((0, group, peer))

    for index in range(AHEAD):
        for copy in in_copies(index):
            copy.start()

    plane, line, side = group // 8, group // 2 % 4, group % 2
    line_mates = [(0, group + ((line + step) % 4 - line) * 2, half) for step in range(1, 4)]
    plane_mates = [(0, group + ((plane + step) % 4 - plane) * 8, half) for step in range(1, 4)]
    side_mate = (0, group + 1 - 2 * side, half)

    def tell(index, device):
        pl.semaphore_signal(known_sem.at[index], inc=1, device_id=device, device_id_type=MESH)

    @pl.when(first)
    def _():
        for device in line_mates + plane_mates + [side_mate, (1, group, half)]:
            greet(device)
        pl.semaphore_wait(barrier, 10)

        for item in range(slots):
            for kind in range(2):
                entry_own(item, kind).start()
            for index in range(CHUNKS):
                for kind in range(2):
                    entry_far(item, kind, index).start()
        for item in range(slots, items):
            entry_own(item, 1).start()
        for device in plane_mates:
            tell(0, device)

        for slot in range(slots):
            @pl.loop(0, groups)
            def _(target):
                origin = jnp.int32(0)
                for source in range(groups):
                    origin = jnp.where(routes[slot, source] == target, source, origin)
                origins[slot, target] = origin

        pl.semaphore_wait(known_sem.at[0], 3)
        tell(1, side_mate)

    @pl.when(second)
    def _():
        pl.semaphore_wait(barrier, 2)

    def project(item):
        slot = item % slots

        @pl.when(first)
        def _():
            @pl.when(item < slots)
            def _():
                entry_own(slot, 0).wait()
            entry_own(item, 1).wait()

        for index in range(CHUNKS):
            cols = pl.ds(index * chunk, chunk)

            @pl.when(first)
            def _():
                @pl.when(item < slots)
                def _():
                    entry_wait(slot, 0, index)
                entry_wait(item, 1, index)

            @pl.when(second)
            def _():
                if index == 0:
                    arrived(rows_in.at[item], keep_recv.at[item])
                arrived(own_sum.at[slot, :, cols], near_recv.at[item, index])
                arrived(far_sum.at[slot, :, cols], far_recv.at[item, index])

                @pl.loop(0, rows // BAND)
                def _(band):
                    span = pl.ds(pl.multiple_of(band * BAND, BAND), BAND)
                    total = own_sum[slot, span, cols].astype(F32) + far_sum[slot, span, cols].astype(F32)
                    rows_in[item, span, cols] = (rows_in[item, span, cols].astype(F32) + total).astype(BF16)

            gain_row = gain[:, cols].astype(F32)

            @pl.loop(0, rows // BAND)
            def _(band):
                span = pl.ds(pl.multiple_of(band * BAND, BAND), BAND)
                x = rows_in[item, span, cols].astype(F32)
                scaled[span] = (x * gain_row).astype(BF16)
                square = x * x
                lanes = square[:, :128]
                for step in range(1, chunk // 128):
                    lanes = lanes + square[:, step * 128:(step + 1) * 128]
                squares[span] = lanes if index == 0 else squares[span] + lanes

            @pl.when(item == 0)
            def _():
                for copy in in_copies(index):
                    copy.wait()
                if index + AHEAD < CHUNKS:
                    for copy in in_copies(index + AHEAD):
                        copy.start()
                else:
                    for other in range(CHUNKS // AHEAD):
                        wo_copy((index + AHEAD - CHUNKS) * (CHUNKS // AHEAD) + other).start()

            depth = pl.ds(index * chunk, chunk)
            for weights, acc in ((wq, acc_q), (wk, acc_k), (wv, acc_v)):
                for start in range(0, weights.shape[1], 512):
                    part = pl.ds(start, 512)
                    product = jnp.dot(scaled[...], weights[depth, part], preferred_element_type=F32)
                    acc[:, part] = product if index == 0 else acc[:, part] + product

        @pl.when(first)
        def _():
            keep_copy(item).start()

        @pl.when(second)
        def _():
            for copy in state_copies(item):
                copy.start()

        @pl.loop(0, rows // BAND)
        def _(band):
            span = pl.ds(pl.multiple_of(band * BAND, BAND), BAND)
            factor = lax.rsqrt(jnp.sum(squares[span], axis=-1, keepdims=True) * (1.0 / width) + EPSILON)
            queries[span] = (acc_q[span] * factor).astype(BF16)
            keys[span] = (acc_k[span] * factor).astype(BF16)
            values[span] = (acc_v[span] * factor).astype(BF16)

    def attend(item):
        length = lengths[item // slots, item % slots]
        query_pos = lax.broadcasted_iota(jnp.int32, (rows, rows), 0)
        key_pos = lax.broadcasted_iota(jnp.int32, (rows, rows), 1)
        visible = (key_pos < mem_rows) | (key_pos - mem_rows < length) & (
            (query_pos < mem_rows) | (key_pos <= query_pos))
        heads = wq.shape[1] // HEAD_SIZE
        kv_heads = wk.shape[1] // HEAD_SIZE
        per = heads // kv_heads
        seen = jnp.concatenate([visible] * per, axis=0)
        for kv in range(kv_heads):
            k = keys[:, kv * HEAD_SIZE:(kv + 1) * HEAD_SIZE]
            v = values[:, kv * HEAD_SIZE:(kv + 1) * HEAD_SIZE]
            q = jnp.concatenate(
                [queries[:, head * HEAD_SIZE:(head + 1) * HEAD_SIZE] for head in range(kv * per, (kv + 1) * per)], axis=0)
            scores = lax.dot_general(q, k, (((1,), (1,)), ((), ())), preferred_element_type=F32)
            scores = jnp.where(seen, scores * HEAD_SIZE ** (-0.5), -1e30)
            weights = jnp.exp(scores - jnp.max(scores, axis=-1, keepdims=True))
            attn = (weights * (1.0 / jnp.sum(weights, axis=-1, keepdims=True))).astype(BF16)
            mixed = jnp.dot(attn, v, preferred_element_type=F32).astype(BF16)
            for step in range(per):
                head = kv * per + step
                attended[:, head * HEAD_SIZE:(head + 1) * HEAD_SIZE] = mixed[step * rows:(step + 1) * rows]

    def emit(item):
        slot = item % slots
        last = item >= items - slots

        @pl.when(item >= slots)
        def _():
            before = item - slots

            @pl.when(first)
            def _():
                for index in range(CHUNKS):
                    far_copy(before, index).wait_send()
                    near_copy(before, index).wait_send()

            @pl.when(second)
            def _():
                for index in range(CHUNKS):
                    mem_all(before, index).wait_send()
                seg_part(before).wait_send()

        for index in range(CHUNKS):
            cols = pl.ds(index * chunk, chunk)

            @pl.when(item == 0)
            def _():
                wo_copy(index).wait()

            partial[slot, :, cols] = jnp.dot(attended[...], wo[:, cols], preferred_element_type=F32).astype(BF16)

            @pl.when(first)
            def _():
                far_copy(item, index).start()
                near_copy(item, index).start()

            @pl.when(second & jnp.logical_not(last))
            def _():
                mem_all(item, index).start()

            @pl.when(second & last)
            def _():
                mem_part(item, index).start()

        @pl.when(second)
        def _():
            seg_part(item).start()

    def add_rows(item, cols, start, landed, count):
        slot = item % slots

        @pl.loop(0, count // BAND)
        def _(band):
            span = pl.ds(pl.multiple_of(start + band * BAND, BAND), BAND)
            there = pl.ds(pl.multiple_of(landed + band * BAND, BAND), BAND)
            total = partial[slot, span, cols].astype(F32) + last_sum[item, there, cols].astype(F32)
            rows_in[item, span, cols] = (rows_in[item, span, cols].astype(F32) + total).astype(BF16)

    def finish_memory(item, slot):
        state = state_copies(item)
        for copy in state:
            copy.wait_send()

        @pl.when(item < items - slots)
        def _():
            if slot == 0:
                pl.semaphore_wait(known_sem.at[2], 1)

            @pl.loop(0, CHUNKS)
            def _(index):
                cols = columns(index)
                arrived(last_sum.at[item, pl.ds(0, mem_rows), cols], mem_recv.at[item, index])
                add_rows(item, cols, 0, 0, mem_rows)

                @pl.loop(0, groups // CHUNKS)
                def _(step):
                    piece_copy(slot, index * (groups // CHUNKS) + step).start()

        @pl.when(item >= items - slots)
        def _():
            @pl.loop(0, CHUNKS)
            def _(index):
                cols = columns(index)
                arrived(last_sum.at[item, pl.ds(0, dev_rows), cols], mem_recv.at[item, index])
                add_rows(item, cols, mem_home, 0, dev_rows)

        out_copy(item, 0).start()

    def finish_segment(item):
        arrived(last_sum.at[item, pl.ds(mem_rows, dev_rows)], seg_recv.at[item])

        @pl.loop(0, CHUNKS)
        def _(index):
            add_rows(item, columns(index), seg_home, mem_rows, dev_rows)

        out_copy(item, 1).start()

    @pl.loop(0, items)
    def _(item):
        @pl.when(first & (item == slots))
        def _():
            reorder(0)

        @pl.when(first & (item == slots + 1))
        def _():
            reorder(1)

        project(item)

        @pl.when(first & (item == 0))
        def _():
            pl.semaphore_wait(known_sem.at[1], 1)
            tell(2, (1, group, half))

        @pl.when(second & (item % slots == 1))
        def _():
            finish_memory(item - 1, 0)

        attend(item)
        emit(item)

        @pl.when(second & (item % slots == 1))
        def _():
            finish_memory(item, 1)
            finish_segment(item - 1)
            finish_segment(item)

    @pl.loop(0, items)
    def _(item):
        last = item >= items - slots

        @pl.when(first)
        def _():
            for source, target in states(item)[:1]:
                arrived(target, state_recv.at[item, 0])
            for source, target in states(item)[1:]:
                arrived(target, state_recv.at[item, 1])
            for index in range(CHUNKS):
                entry_far(item, 1, index).wait_send()
            keep_copy(item).wait_send()

            @pl.when(last)
            def _():
                for index in range(CHUNKS):
                    far_copy(item, index).wait_send()
                    near_copy(item, index).wait_send()

        @pl.when(second)
        def _():
            out_copy(item, 0).wait()
            out_copy(item, 1).wait()

            @pl.when(last)
            def _():
                for index in range(CHUNKS):
                    mem_part(item, index).wait_send()
                seg_part(item).wait_send()

    for slot in range(slots):
        @pl.when(first)
        def _():
            for index in range(CHUNKS):
                entry_far(slot, 0, index).wait_send()
            arrived(picked.at[slot, pl.ds(0, groups - 1)], back_send.at[slot])

        @pl.when(second)
        def _():
            arrived(spread[slot], route_send.at[slot])


def run_window(segments, memory, lengths, routes, gain, w_query, w_key, w_value, w_out):
    rounds, slots, dev_rows, width = segments.shape
    items = rounds * slots
    mem_rows = 2 * dev_rows
    rows = 2 * mem_rows
    groups = width // PIECE
    dma = pltpu.SemaphoreType.DMA
    vmem = pltpu.VMEM
    states = jax.ShapeDtypeStruct((1, rounds, slots, dev_rows, width), BF16)
    q_width, kv_width = w_query.shape[2], w_key.shape[2]
    return pl.pallas_call(
        window_kernel,
        out_shape=(states, states),
        in_specs=[pl.BlockSpec(memory_space=pl.ANY)] * 2
        + [pl.BlockSpec(memory_space=pltpu.SMEM)] * 2
        + [pl.BlockSpec(memory_space=vmem)]
        + [pl.BlockSpec(memory_space=pl.ANY)] * 4,
        out_specs=(pl.BlockSpec(memory_space=pl.ANY), pl.BlockSpec(memory_space=pl.ANY)),
        scratch_shapes=[
            vmem(w_query.shape[1:], BF16),
            vmem(w_key.shape[1:], BF16),
            vmem(w_value.shape[1:], BF16),
            vmem(w_out.shape[1:], BF16),
            vmem((items, rows, width), BF16),
            vmem((slots, rows, width), BF16),
            vmem((slots, rows, width), BF16),
            vmem((slots, rows, width), BF16),
            vmem((items, mem_rows + dev_rows, width), BF16),
            vmem((rows, width // CHUNKS), BF16),
            vmem((rows, 128), F32),
            vmem((rows, q_width), F32),
            vmem((rows, kv_width), F32),
            vmem((rows, kv_width), F32),
            vmem((rows, q_width), BF16),
            vmem((rows, kv_width), BF16),
            vmem((rows, kv_width), BF16),
            vmem((rows, q_width), BF16),
            vmem((groups, mem_rows, PIECE), BF16),
            vmem((groups, mem_rows, PIECE), BF16),
            vmem((slots, groups, mem_rows, PIECE), BF16),
            pltpu.SMEM((slots, groups), jnp.int32),
            dma((CHUNKS, 3)),
            dma((CHUNKS,)),
            dma((items, 2)),
            dma((items, 2, CHUNKS)),
            dma((items, 2, CHUNKS)),
            dma((items,)),
            dma((items,)),
            dma((items, CHUNKS)),
            dma((items, CHUNKS)),
            dma((items, CHUNKS)),
            dma((items, CHUNKS)),
            dma((items, CHUNKS)),
            dma((items, CHUNKS)),
            dma((items,)),
            dma((items,)),
            dma((items, 2)),
            dma((items, 2)),
            dma((items, 2)),
            dma((slots,)),
            dma((slots,)),
            dma((slots,)),
            dma((slots,)),
            pltpu.SemaphoreType.REGULAR((3,)),
        ],
        compiler_params=pltpu.CompilerParams(
            collective_id=0, has_side_effects=True, vmem_limit_bytes=63 * 1024 * 1024
        ),
    )(segments, memory, lengths, routes, gain, w_query, w_key, w_value, w_out)


def place_kernel(mem, seg, mem_out, seg_out, held, in_sem, sem):
    spots = [(kind, rnd, slot) for kind in range(2) for rnd in range(mem.shape[1]) for slot in range(mem.shape[2])]
    ins, outs = [], []
    for kind, rnd, slot in spots:
        source, target = ((mem, mem_out), (seg, seg_out))[kind]
        ins.append(pltpu.make_async_copy(source.at[0, rnd, slot], held.at[kind, rnd, slot], in_sem.at[kind, rnd, slot]))
        outs.append(pltpu.make_async_copy(held.at[kind, rnd, slot], target.at[0, rnd, slot], sem.at[kind, rnd, slot]))
    for copy in ins:
        copy.start()
    for into, out in zip(ins, outs):
        into.wait()
        out.start()
    for out in outs:
        out.wait()


def place(mem, seg):
    anywhere = pl.BlockSpec(memory_space=pl.ANY)
    states = jax.ShapeDtypeStruct(mem.shape, mem.dtype)
    return pl.pallas_call(
        place_kernel,
        out_shape=(states, states),
        in_specs=[anywhere, anywhere],
        out_specs=(anywhere, anywhere),
        scratch_shapes=[
            pltpu.VMEM((2,) + mem.shape[1:], mem.dtype),
            pltpu.SemaphoreType.DMA((2,) + mem.shape[1:3]),
            pltpu.SemaphoreType.DMA((2,) + mem.shape[1:3]),
        ],
        compiler_params=pltpu.CompilerParams(vmem_limit_bytes=16 * 1024 * 1024),
    )(mem, seg)


def per_device(segments, memory_in, seg_lengths, routes, w_query, w_key, value_weight, w_out, norm_gain):
    mem, seg = run_window(
        segments, memory_in, seg_lengths, routes, norm_gain, w_query, w_key, value_weight, w_out)
    return place(mem, seg)


def solution(mesh):
    return jax.shard_map(
        per_device,
        mesh=mesh,
        in_specs=(
            P(None, "dp", "mp", None),
            P("dp", "mp", None),
            P(None, "dp"),
            P(),
            P("phase", None, "mp"),
            P("phase", None, "mp"),
            P("phase", None, "mp"),
            P("phase", "mp", None),
            P("phase", None),
        ),
        out_specs=(P("phase", None, "dp", "mp", None), P("phase", None, "dp", "mp", None)),
        check_vma=False,
    )
```

time: 796 us -> 143 us (0.18); the launches traced: 786 us -> 142 us
  waiting for transfers between devices: 404 us -> 0 us
  matrix products: 183 us -> 0 us
  Pallas kernels: 0 us -> 139 us
  blocking collectives: 89 us -> 0 us
  other arithmetic: 46.6 us -> 0 us
  starting transfers between devices: 29.3 us -> 0 us
  local copies, waits for them, and re-layouts: 19.3 us -> 2.44 us
  between operations: 15.1 us -> 0.65 us
    all_to_all x2 -> x0, waiting for transfers between devices: 245 us -> none  [route_memory(): lax.all_to_all(outgoing, 'dp', split_axis=0, concat_axis=0, tiled=True)]
    dot_general x35 -> x0, matrix products: 174 us -> none  [the longest x5 44.3 us: section_layer(): jnp.dot(normed, w_query, preferred_element_type=jnp.float32)]
    reduce_scatter x5 -> x0, waiting for transfers between devices: 154 us -> none  [section_layer(): lax.psum_scatter(jnp.concatenate([term_mem, term_seg], axis=1).reshape(bl...]
    pallas_call x0 -> x2, Pallas kernels: none -> 139 us  [the longest x1 138 us: run_window(): pl.pallas_call(window_kernel, out_shape=(states, states), in_specs=[pl.Bl...]
    all_gather x10 -> x0, blocking collectives: 89 us -> none  [the longest x5 46.9 us: section_layer(): lax.all_gather(norm_rows(mem_x, gain), 'mp', axis=0, tiled=True)]
    reduce_sum x13 -> x0, other arithmetic: 18.2 us -> none  [the longest x2 10.4 us: route_memory(): return jnp.sum(received.astype(jnp.float32), axis=0).astype(jnp.bfloat16)]
    all_to_all x2 -> x0, starting transfers between devices: 14.2 us -> none  [route_memory(): lax.all_to_all(outgoing, 'dp', split_axis=0, concat_axis=0, tiled=True)]
    reshape x15 -> x0, local copies, waits for them, and re-layouts: 13.1 us -> none  [the longest x5 9.14 us: section_layer(): heads_of_query.reshape(rows_total, kv_dev, per_group, HEAD_SIZE)]
  transfers between devices with their start and end apart: 15 -> 0, of which waited for: 14 -> 0; matrix products, arithmetic and copies ran while one was open for 1% -> 0% of each run, Pallas kernels for 0% -> 0%
where the time goes in v3:
time: 143 us; the launch traced here: 142 us
  Pallas kernels  139 us (97%)
  local copies, waits for them, and re-layouts  2.44 us (2%)
    pallas_call x1, Pallas kernels, run_window(): pl.pallas_call(window_kernel, out_shape=(states, states), in_specs=[pl.Bl...  138 us

profile of v3, /device:TPU:1, one launch (start us, length us, event | category | flops | bytes accessed | tf_op | source)
XLA Modules:
  0.0 142.5 jit_solution(13855048046376216143)
XLA Ops:
  0.6 137.8 %shard_map.104 = (bf16[1,2,2,32,4096]{4,3,2,1,0:T(8,128)(2,1)}, bf16[1,2,2,32,4096]{4,3,2,1,0:T(8,128)(2,1)}) custom-call(bf16[2,2,32,4096]{3,2,1,0:T(8,128)(2,1)} %segments.1, bf16[2,32,4096]{2,1,0:T(8,128)(2,1)} %memory.1, s32[2,2]{1,0:T(2,128)} %lengths.1, s32[2,32]{1,0:T(2,128)} %routes.1, bf16[1,4096]{1,0:T(2,128)(2,1)} %gain.1, ...), custom_call_target="tpu_custom_call" | custom-call | tf_op jit(solution)/shard_map/pallas_call | solution.py:486
  138.4 0.0 copy-start
  138.4 1.2 copy-done
  139.6 0.0 copy-start.1
  139.6 1.2 copy-done.1
  140.9 1.6 %shard_map.105 = (bf16[1,2,2,32,4096]{4,3,2,1,0:T(8,128)(2,1)}, bf16[1,2,2,32,4096]{4,3,2,1,0:T(8,128)(2,1)}) custom-call(bf16[1,2,2,32,4096]{4,3,2,1,0:T(8,128)(2,1)S(1)} %copy-done, bf16[1,2,2,32,4096]{4,3,2,1,0:T(8,128)(2,1)S(1)} %copy-done.1), custom_call_target="tpu_custom_call" | custom-call | tf_op jit(solution)/shard_map/pallas_call | solution.py:566
Async XLA Ops:
  138.4 1.2 copy-start
  139.6 1.2 copy-start.1

commit v4 on v3

--- a/solution.py
+++ b/solution.py
@@ -131,8 +131,6 @@
     def reorder(slot):
         item = slots + slot
         arrived(spread[slot], route_recv.at[slot])
-        for index in range(CHUNKS):
-            entry_far(item, 1, index).start()
         rows_in[item, pl.ds(0, mem_rows), own_piece] = spread[slot][origins[slot, group]]
 
         @pl.loop(1, groups)
@@ -142,6 +140,8 @@
             remote(picked.at[slot, target], rows_in.at[item, pl.ds(0, mem_rows), own_piece],
                    back_send.at[slot], back_recv.at[slot], (0, target, half)).start()
 
+        for index in range(CHUNKS):
+            entry_far(item, 1, index).start()
         arrived(picked.at[slot, pl.ds(0, groups - 1)], back_recv.at[slot])
 
     barrier = pltpu.get_barrier_semaphore()
@@ -177,9 +177,9 @@
         for item in range(slots):
             for kind in range(2):
                 entry_own(item, kind).start()
-            for index in range(CHUNKS):
-                for kind in range(2):
-                    entry_far(item, kind, index).start()
+        for index in range(CHUNKS):
+            for kind in range(2):
+                entry_far(0, kind, index).start()
         for item in range(slots, items):
             entry_own(item, 1).start()
         for device in plane_mates:
@@ -219,6 +219,13 @@
                 def _():
                     entry_wait(slot, 0, index)
                 entry_wait(item, 1, index)
+                if index == CHUNKS // 2:
+                    @pl.when(item == 0)
+                    def _():
+                        for other in range(1, slots):
+                            for ahead in range(CHUNKS):
+                                for kind in range(2):
+                                    entry_far(other, kind, ahead).start()
 
             @pl.when(second)
             def _():
@@ -573,7 +580,7 @@
             pltpu.SemaphoreType.DMA((2,) + mem.shape[1:3]),
             pltpu.SemaphoreType.DMA((2,) + mem.shape[1:3]),
         ],
-        compiler_params=pltpu.CompilerParams(vmem_limit_bytes=16 * 1024 * 1024),
+        compiler_params=pltpu.CompilerParams(vmem_limit_bytes=63 * 1024 * 1024),
     )(mem, seg)
 
 

time: 143 us -> 135 us (0.944)
  Pallas kernels: 139 us -> 134 us
  local copies, waits for them, and re-layouts: 2.44 us -> 0 us
    pallas_call x1, Pallas kernels: 138 us -> 132 us  [run_window(): pl.pallas_call(window_kernel, out_shape=(states, states), in_specs=[pl.Bl...]
    unnamed x4 -> x0, local copies, waits for them, and re-layouts: 2.44 us -> none
where the time goes in v4:
time: 135 us
  Pallas kernels  134 us (99%)
    pallas_call x1, Pallas kernels, run_window(): pl.pallas_call(window_kernel, out_shape=(states, states), in_specs=[pl.Bl...  132 us

profile of v4, /device:TPU:1, one launch (start us, length us, event | category | flops | bytes accessed | tf_op | source)
XLA Modules:
  0.0 134.9 jit_solution(13783476323331255020)
XLA Ops:
  0.6 131.9 %shard_map.104 = (bf16[1,2,2,32,4096]{4,3,2,1,0:T(8,128)(2,1)}, bf16[1,2,2,32,4096]{4,3,2,1,0:T(8,128)(2,1)}) custom-call(bf16[2,2,32,4096]{3,2,1,0:T(8,128)(2,1)} %segments.1, bf16[2,32,4096]{2,1,0:T(8,128)(2,1)} %memory.1, s32[2,2]{1,0:T(2,128)} %lengths.1, s32[2,32]{1,0:T(2,128)} %routes.1, bf16[1,4096]{1,0:T(2,128)(2,1)} %gain.1, ...), custom_call_target="tpu_custom_call" | custom-call | tf_op jit(solution)/shard_map/pallas_call | solution.py:493
  132.6 2.4 %shard_map.105 = (bf16[1,2,2,32,4096]{4,3,2,1,0:T(8,128)(2,1)}, bf16[1,2,2,32,4096]{4,3,2,1,0:T(8,128)(2,1)}) custom-call(bf16[1,2,2,32,4096]{4,3,2,1,0:T(8,128)(2,1)} %get-tuple-element.4.mem, bf16[1,2,2,32,4096]{4,3,2,1,0:T(8,128)(2,1)} %get-tuple-element.5.seg), custom_call_target="tpu_custom_call" | custom-call | tf_op jit(solution)/shard_map/pallas_call | solution.py:573

commit v5 on v4

--- a/solution.py
+++ b/solution.py
@@ -354,7 +354,7 @@
             def _():
                 mem_part(item, index).start()
 
-        @pl.when(second)
+        @pl.when(second & last)
         def _():
             seg_part(item).start()
 
@@ -417,6 +417,10 @@
         def _():
             reorder(1)
 
+        @pl.when(second & (item == 1))
+        def _():
+            finish_memory(item - 1, 0)
+
         project(item)
 
         @pl.when(first & (item == 0))
@@ -424,16 +428,22 @@
             pl.semaphore_wait(known_sem.at[1], 1)
             tell(2, (1, group, half))
 
-        @pl.when(second & (item % slots == 1))
-        def _():
-            finish_memory(item - 1, 0)
-
         attend(item)
         emit(item)
 
+        @pl.when(second & (item == items - 1))
+        def _():
+            finish_memory(item - 1, 0)
+
         @pl.when(second & (item % slots == 1))
         def _():
             finish_memory(item, 1)
+
+            @pl.when(item < items - slots)
+            def _():
+                seg_part(item - 1).start()
+                seg_part(item).start()
+
             finish_segment(item - 1)
             finish_segment(item)
 

time: 135 us -> 133 us (0.985)
  Pallas kernels: 134 us -> 132 us
    pallas_call x1, Pallas kernels: 132 us -> 130 us  [run_window(): pl.pallas_call(window_kernel, out_shape=(states, states), in_specs=[pl.Bl...]
where the time goes in v5:
time: 133 us
  Pallas kernels  132 us (99%)
    pallas_call x1, Pallas kernels, run_window(): pl.pallas_call(window_kernel, out_shape=(states, states), in_specs=[pl.Bl...  130 us

profile of v5, /device:TPU:1, one launch (start us, length us, event | category | flops | bytes accessed | tf_op | source)
XLA Modules:
  0.0 132.8 jit_solution(1790931807582358958)
XLA Ops:
  0.6 129.7 %shard_map.104 = (bf16[1,2,2,32,4096]{4,3,2,1,0:T(8,128)(2,1)}, bf16[1,2,2,32,4096]{4,3,2,1,0:T(8,128)(2,1)}) custom-call(bf16[2,2,32,4096]{3,2,1,0:T(8,128)(2,1)} %segments.1, bf16[2,32,4096]{2,1,0:T(8,128)(2,1)} %memory.1, s32[2,2]{1,0:T(2,128)} %lengths.1, s32[2,32]{1,0:T(2,128)} %routes.1, bf16[1,4096]{1,0:T(2,128)(2,1)} %gain.1, ...), custom_call_target="tpu_custom_call" | custom-call | tf_op jit(solution)/shard_map/pallas_call | solution.py:503
  130.4 2.4 %shard_map.105 = (bf16[1,2,2,32,4096]{4,3,2,1,0:T(8,128)(2,1)}, bf16[1,2,2,32,4096]{4,3,2,1,0:T(8,128)(2,1)}) custom-call(bf16[1,2,2,32,4096]{4,3,2,1,0:T(8,128)(2,1)} %get-tuple-element.4.mem, bf16[1,2,2,32,4096]{4,3,2,1,0:T(8,128)(2,1)} %get-tuple-element.5.seg), custom_call_target="tpu_custom_call" | custom-call | tf_op jit(solution)/shard_map/pallas_call | solution.py:583

commit v6 on v5

--- a/solution.py
+++ b/solution.py
@@ -354,7 +354,7 @@
             def _():
                 mem_part(item, index).start()
 
-        @pl.when(second & last)
+        @pl.when(second & (item == items - 1))
         def _():
             seg_part(item).start()
 
@@ -422,6 +422,10 @@
             finish_memory(item - 1, 0)
 
         project(item)
+
+        @pl.when(second & (item == items - 1))
+        def _():
+            seg_part(item - 1).start()
 
         @pl.when(first & (item == 0))
         def _():

time: 133 us -> 134 us (level)
  no operation moved by 1% of the time
where the time goes in v6:
time: 134 us
  Pallas kernels  133 us (99%)
    pallas_call x1, Pallas kernels, run_window(): pl.pallas_call(window_kernel, out_shape=(states, states), in_specs=[pl.Bl...  131 us

profile of v6, /device:TPU:1, one launch (start us, length us, event | category | flops | bytes accessed | tf_op | source)
XLA Modules:
  0.0 133.8 jit_solution(15860778986609963545)
XLA Ops:
  0.6 130.7 %shard_map.104 = (bf16[1,2,2,32,4096]{4,3,2,1,0:T(8,128)(2,1)}, bf16[1,2,2,32,4096]{4,3,2,1,0:T(8,128)(2,1)}) custom-call(bf16[2,2,32,4096]{3,2,1,0:T(8,128)(2,1)} %segments.1, bf16[2,32,4096]{2,1,0:T(8,128)(2,1)} %memory.1, s32[2,2]{1,0:T(2,128)} %lengths.1, s32[2,32]{1,0:T(2,128)} %routes.1, bf16[1,4096]{1,0:T(2,128)(2,1)} %gain.1, ...), custom_call_target="tpu_custom_call" | custom-call | tf_op jit(solution)/shard_map/pallas_call | solution.py:507
  131.4 2.4 %shard_map.105 = (bf16[1,2,2,32,4096]{4,3,2,1,0:T(8,128)(2,1)}, bf16[1,2,2,32,4096]{4,3,2,1,0:T(8,128)(2,1)}) custom-call(bf16[1,2,2,32,4096]{4,3,2,1,0:T(8,128)(2,1)} %get-tuple-element.4.mem, bf16[1,2,2,32,4096]{4,3,2,1,0:T(8,128)(2,1)} %get-tuple-element.5.seg), custom_call_target="tpu_custom_call" | custom-call | tf_op jit(solution)/shard_map/pallas_call | solution.py:587
